TPU v7x, 32 devices: a whole 2x2x4 slice. The times are simulated.
32 devices in a mesh: dp: 8 (over z, x), tensor: 4 (over y, core).
Axes of the slice: x: 2, y: 2, z: 4, core: 2. Of those that a mesh axis runs over, the one named last changes fastest.
Arguments:
- hidden: bfloat16 [2048, 1024], P('dp'), may hold values from -6 to 6
- positions: int32 [2048], P('dp'), may hold values from 0 to 255, as said below
- out_grad: bfloat16 [2048, 1024], P('dp'), may hold values from -6 to 6
- norm_one: float32 [1024], replicated, may hold values from 0.5 to 1.5
- zx_weight: bfloat16 [1024, 2, 1536], P(None, None, 'tensor'), may hold values from -0.1875 to 0.1875
- bc_weight: bfloat16 [1024, 256], replicated, may hold values from -0.1875 to 0.1875
- dt_weight: bfloat16 [1024, 24], P(None, 'tensor'), may hold values from -0.1875 to 0.1875
- conv_inner: float32 [5, 1536], P(None, 'tensor'), may hold values from -0.5 to 0.5
- conv_state: float32 [5, 256], replicated, may hold values from -0.5 to 0.5
- decay_log: float32 [24], P('tensor'), may hold values from 0 to 2.77
- dt_bias: float32 [24], P('tensor'), may hold values from -6 to -2
- skip_gain: float32 [24], P('tensor'), may hold values from 0.5 to 1.5
- gated_gain: float32 [1536], P('tensor'), may hold values from 0.5 to 1.5
- out_weight: bfloat16 [1536, 1024], P('tensor'), may hold values from -0.15625 to 0.15625
- q_weight: bfloat16 [1024, 512], P(None, 'tensor'), may hold values from -0.1875 to 0.1875
- kv_weight: bfloat16 [1024, 2, 128], replicated, may hold values from -0.1875 to 0.1875
- o_weight: bfloat16 [512, 1024], P('tensor'), may hold values from -1 to 1
- norm_two: float32 [1024], replicated, may hold values from 0.5 to 1.5
- gu_weight: bfloat16 [1024, 2, 2048], P(None, None, 'tensor'), may hold values from -0.1875 to 0.1875
- down_weight: bfloat16 [2048, 1024], P('tensor'), may hold values from -0.125 to 0.125
Outputs:
- layer_out: bfloat16 [2048, 1024], P('dp')
- input_grad: bfloat16 [2048, 1024], P('dp')
- norm_one_grad: float32 [1024], replicated
- zx_grad: float32 [1024, 2, 1536], P('dp', None, 'tensor')
- bc_grad: float32 [1024, 256], P('dp')
- dt_grad: float32 [1024, 24], P('dp', 'tensor')
- conv_inner_grad: float32 [5, 1536], P(None, 'tensor')
- conv_state_grad: float32 [5, 256], replicated
- decay_log_grad: float32 [24], P('tensor')
- dt_bias_grad: float32 [24], P('tensor')
- skip_gain_grad: float32 [24], P('tensor')
- gated_gain_grad: float32 [1536], P('tensor')
- out_weight_grad: float32 [1536, 1024], P('tensor', 'dp')
- q_grad: float32 [1024, 512], P('dp', 'tensor')
- kv_grad: float32 [1024, 2, 128], P('dp')
- o_weight_grad: float32 [512, 1024], P('tensor', 'dp')
- norm_two_grad: float32 [1024], replicated
- gu_grad: float32 [1024, 2, 2048], P('dp', None, 'tensor')
- down_grad: float32 [2048, 1024], P('tensor', 'dp')
Inputs may be any that keep to these rules, and one draw needn't show every extreme that they name: `positions`: each sequence of 256 tokens holds whole documents; a position counts from 0 at a document's first token, and every sequence begins a document; the first sequence is one document.
All inputs are finite; a program needn't handle non-finite values.
Results may differ from a plain program's by a relative error of at most 0.012.
Values sent between devices are 32-bit elements; how exact they have to be, the bound alone decides.
No kernel may reach another device: no remote copies, remote signals or barrier semaphores. Data moves between devices by JAX's collectives and lax.ppermute only.
A program may use at most 128 MiB of HBM per device.

v0:
```python
import functools

import jax
import jax.numpy as jnp
from jax import lax
from jax.experimental import pallas as pl
from jax.experimental.pallas import tpu as pltpu
from jax.sharding import PartitionSpec as P

QH = 8
KVH = 2
HD = 64
HEAD_PAD = 128
STATE_ROWS = 18
STATE_PAD = 24
SMALL_ROWS = 16
COST = 3 * 10**9

epsilon = 1e-05
rope_base = 10000.0
highest = lax.Precision.HIGHEST
bf16 = jnp.bfloat16
f32 = jnp.float32
params = pltpu.CompilerParams(vmem_limit_bytes=40 * 1024 * 1024)


def dot(left, right, dims, precision=None):
    return lax.dot_general(
        left,
        right,
        ((dims[:1], dims[1:]), ((), ())),
        precision=precision,
        preferred_element_type=f32,
    )


def rms_scale(values):
    return lax.rsqrt(jnp.mean(values * values, axis=-1, keepdims=True) + epsilon)


def sigmoid(values):
    return 1.0 / (1.0 + jnp.exp(-values))


def rounded(values):
    return values.astype(bf16).astype(f32)


def cost(flops, read, exps=0):
    return pl.CostEstimate(flops=COST, bytes_accessed=10**6, transcendentals=0)


def call(kernel, name, out_shapes, values, ahead=(), scratch=(), flops=10**6):
    def place(value):
        if value.dtype == jnp.int32 and value.size == 1:
            return pl.BlockSpec(memory_space=pltpu.SMEM)
        return whole(value)

    def whole(value):
        zeros = (0,) * len(value.shape)
        return pl.BlockSpec(value.shape, lambda step: zeros)

    shapes = [jax.ShapeDtypeStruct(shape, kind) for shape, kind in out_shapes]
    return pl.pallas_call(
        kernel,
        grid=(1,),
        in_specs=[place(value) for value in values]
        + [pl.BlockSpec(memory_space=pl.ANY)] * len(ahead),
        out_specs=[whole(shape) for shape in shapes],
        out_shape=shapes,
        scratch_shapes=[pltpu.VMEM(shape, kind) for shape, kind in scratch],
        compiler_params=params,
        cost_estimate=cost(flops, flops),
        name=name,
    )(*values, *ahead)


def swap(values, axis, mask):
    pairs = [(index, index ^ mask) for index in range(lax.axis_size(axis))]
    return lax.ppermute(values, axis, pairs)


def spread_tensor(values):
    return [values] + [swap(values, "tensor", mask) for mask in (1, 2, 3)]


def add_spread(parts):
    return (parts[0] + parts[1]) + (parts[2] + parts[3])


def add_kernel(left_ref, right_ref, *rest):
    rest[-1][...] = left_ref[...] + right_ref[...]


def tensor_halves(mine, ahead=()):
    values = (mine, swap(mine, "tensor", 2))
    (mine,) = call(add_kernel, "add_halves", [(mine.shape, f32)], values, ahead)
    return mine, swap(mine, "tensor", 1)


def swap_shared(values, mask):
    first = swap(values, "dp", mask)
    return first, swap(first, "tensor", 1)


def rows(values, start, size):
    return lax.dynamic_slice_in_dim(values, start, size, 0)


def half_rows(core, size):
    return pl.ds(pl.multiple_of(core * size, size), size)


def halving_order(size, pair):
    order, bits, bit = [0], [], 1
    while bit < size:
        if bit != pair:
            bits.append(bit)
        bit *= 2
    for bit in reversed(bits):
        order = [index ^ bit for index in order] + order
    return order, bits


def pick_blocks(values, offsets):
    width = values.shape[1] // lax.axis_size("dp")
    me = lax.axis_index("dp")
    return jnp.concatenate(
        [
            lax.dynamic_slice_in_dim(values, (me ^ offset) * width, width, 1)
            for offset in offsets
        ],
        axis=1,
    )


def arrange_kernel(order, pair, width, me_ref, *refs):
    count = len(refs) // 2
    me = me_ref[0]
    half = refs[-1].shape[0]
    span = half_rows(me_ref[1], half)
    partner_ref = refs[-1]
    for index in range(count):
        value_ref, own_ref = refs[index], refs[count + index]
        base = index * len(order) * width
        for place, offset in enumerate(order):
            cols = pl.ds(pl.multiple_of((me ^ offset) * width, 128), width)
            own_ref[:, place * width : (place + 1) * width] = value_ref[:, cols].astype(bf16)
            cols = pl.ds(pl.multiple_of((me ^ offset ^ pair) * width, 128), width)
            start = base + place * width
            partner_ref[:, start : start + width] = value_ref[span, cols].astype(f32)


def arrange(pair, *arrays):
    size = lax.axis_size("dp")
    order, _ = halving_order(size, pair)
    tokens, model = arrays[0].shape
    width = model // size
    half = len(order) * width
    if width % 128:
        partner = [index ^ pair for index in order]
        start = lax.axis_index("tensor") % 2 * (tokens // 2)
        sent = [
            rows(pick_blocks(values, partner), start, tokens // 2).astype(f32) for values in arrays
        ]
        return [pick_blocks(values, order) for values in arrays] + [
            jnp.concatenate(sent, axis=1)
        ]
    vmem = pl.BlockSpec(memory_space=pltpu.VMEM)
    me = jnp.stack([lax.axis_index("dp"), lax.axis_index("tensor") % 2]).astype(jnp.int32)
    return pl.pallas_call(
        functools.partial(arrange_kernel, order, pair, width),
        in_specs=[pl.BlockSpec(memory_space=pltpu.SMEM)] + [vmem] * len(arrays),
        out_shape=[jax.ShapeDtypeStruct((tokens, half), bf16) for _ in arrays]
        + [jax.ShapeDtypeStruct((tokens // 2, half * len(arrays)), f32)],
        compiler_params=params,
        cost_estimate=cost(10**6, 8 * tokens * model),
        name="arrange",
    )(me, *arrays)


def pair_product_kernel(low, high, starts, blocks_first, core_ref, *refs):
    own_ref, got_ref, other_ref, side_ref, side_got_ref = refs[:5]
    out_ref, joined_ref = refs[-2:]
    half = got_ref.shape[0]
    tokens = 2 * half
    core = core_ref[0]
    joined_ref[half_rows(core, half), :] = got_ref[:, low:high].astype(bf16)
    joined_ref[half_rows(1 - core, half), :] = other_ref[:, low:high].astype(bf16)
    side_cols = side_ref.shape[1]
    chunk = 384 if side_cols % 384 == 0 else 512 if side_cols % 512 == 0 else side_cols
    added = refs[5 : 5 + len(starts)]
    for at in range(0, side_cols, chunk):
        cols = slice(at, at + chunk)
        total = None
        for block, ref in ((own_ref[:, low:high], side_ref), (joined_ref[...], side_got_ref)):
            side = ref[:tokens, cols].astype(bf16)
            if blocks_first:
                term = dot(block, side, (0, 0))
            else:
                term = dot(side, block, (0, 0))
            total = term if total is None else total + term
        for start, ref in zip(starts, added):
            if blocks_first:
                total = total + ref[low - start : high - start, cols]
            else:
                total = total + ref[cols, low - start : high - start]
        if blocks_first:
            out_ref[: high - low, cols] = total
        else:
            out_ref[cols, :] = total
    if side_ref.shape[0] > tokens:
        extra = side_ref[tokens:, :] + side_got_ref[tokens:, :]
        for ref in added:
            extra = extra + ref[ref.shape[0] - extra.shape[0] :, :]
        out_ref[high - low :, :] = extra


def pair_product(blocks, sides, low, high, received, blocks_first, ahead):
    width = high - low
    rows_in, side_cols = sides[0].shape
    tokens = blocks[0].shape[0]
    extra = rows_in - tokens
    core = (lax.axis_index("tensor") % 2).astype(jnp.int32).reshape(1)
    if low % 128 or high % 128 or any(start % 128 for start, _ in received):
        blocks = [block[:, low:high] for block in blocks]
        cut = []
        for start, values in received:
            if blocks_first:
                tail = values[values.shape[0] - extra :]
                values = jnp.concatenate([values[low - start : high - start], tail], axis=0)
            else:
                values = values[:, low - start : high - start]
            cut.append((0, values))
        received, low, high = cut, 0, width
    shape = (width + extra, side_cols) if blocks_first else (side_cols, width)
    starts = tuple(start for start, _ in received)
    (total,) = call(
        functools.partial(pair_product_kernel, low, high, starts, blocks_first),
        "pair_product",
        [(shape, f32)],
        (core, *blocks, *sides, *[value for _, value in received]),
        ahead,
        [((tokens, width), bf16)],
    )
    return total


def halving(blocks, sides, blocks_first, pair=1):
    order, bits = halving_order(lax.axis_size("dp"), pair)
    width = blocks[0].shape[1] // len(order)
    low, high = 0, len(order)
    received = []
    ahead = yield None
    for bit in bits + [0]:
        middle = (low + high) // 2 if bit else high
        value = pair_product(
            blocks, sides, low * width, middle * width, received, blocks_first, ahead or ()
        )
        got = value
        if bit:
            got = swap(value, "dp", bit)
            received.append((middle * width, got))
        low = middle
        ahead = yield value, got


def as_row(values):
    ones = jnp.ones((8, values.shape[1]), f32)
    return dot(ones, values, (1, 1), highest)[0:1]


def as_column(row):
    length = row.shape[1]
    down = lax.broadcasted_iota(jnp.int32, (length, length), 0)
    across = lax.broadcasted_iota(jnp.int32, (length, length), 1)
    return jnp.sum(jnp.where(down == across, row, 0.0), axis=1, keepdims=True)


def sum_column(refs):
    return as_column((refs[0][...] + refs[1][...]) + (refs[2][...] + refs[3][...]))


def conv_values(values, taps, positions):
    total = taps[4:5] + taps[0:1] * values
    for offset in range(1, 4):
        shifted = pltpu.roll(values, offset, 0)
        total = total + taps[offset : offset + 1] * jnp.where(positions >= offset, shifted, 0.0)
    return total


def conv_back(grad, values, taps, positions):
    total = taps[0:1] * grad
    tap_grads = [jnp.sum(grad * values, axis=0, keepdims=True)]
    for offset in range(1, 4):
        masked = jnp.where(positions >= offset, grad, 0.0)
        shifted = pltpu.roll(masked, masked.shape[0] - offset, 0)
        total = total + taps[offset : offset + 1] * shifted
        tap_grads.append(jnp.sum(shifted * values, axis=0, keepdims=True))
    tap_grads.append(jnp.sum(grad, axis=0, keepdims=True))
    return total, tap_grads


def scan_parts(step_in, decay_row, bias_row):
    raw = step_in + bias_row
    step = jnp.maximum(raw, 0.0) + jnp.log(1.0 + jnp.exp(-jnp.abs(raw)))
    rates = -jnp.exp(decay_row) * step
    length = rates.shape[0]
    row = lax.broadcasted_iota(jnp.int32, (length, length), 0)
    col = lax.broadcasted_iota(jnp.int32, (length, length), 1)
    lower = (row >= col).astype(f32)
    upper = (row <= col).astype(f32)
    cumulative = dot(lower, rates, (1, 0), highest)
    cumulative_t = dot(rates, upper, (0, 0), highest)
    return raw, step, rates, cumulative, cumulative_t, row >= col, upper


def scan_forward_kernel(
    zx_ref, bc_ref, dt_ref, taps_x_ref, taps_bc_ref, heads_ref, pos_ref, seg_col_ref, seg_row_ref,
    y_ref, gated_ref, square_ref, xa_ref, ba_ref,
):
    positions = pos_ref[...]
    conv_x = conv_values(zx_ref[1], taps_x_ref[...], positions)
    x_act = conv_x * sigmoid(conv_x)
    conv_bc = conv_values(bc_ref[...], taps_bc_ref[...], positions)
    bc_act = (conv_bc * sigmoid(conv_bc)).astype(bf16)
    state = bc_act.shape[1] // 2
    xa_ref[...] = x_act
    ba_ref[...] = bc_act
    heads = heads_ref[...]
    _, step, _, cumulative, cumulative_t, causal, _ = scan_parts(
        dt_ref[...], heads[0:1], heads[1:2]
    )
    inside = causal & (seg_col_ref[...] == seg_row_ref[...])
    gram = dot(bc_act[:, state:], bc_act[:, :state], (1, 1))
    length = positions.shape[0]
    lane = lax.broadcasted_iota(jnp.int32, (length, 128), 1)
    low_half = lane < 64
    square = jnp.zeros((length, 128), f32)
    for pair in range(x_act.shape[1] // 128):
        cols = slice(pair * 128, pair * 128 + 128)
        first, second = 2 * pair, 2 * pair + 1
        x_pair = x_act[:, cols]
        dt_pair = jnp.where(low_half, step[:, first : first + 1], step[:, second : second + 1])
        scaled = x_pair * dt_pair
        total = jnp.where(
            low_half, heads[2:3, first : first + 1], heads[2:3, second : second + 1]
        ) * x_pair
        for head, keep in ((first, low_half), (second, ~low_half)):
            gap = cumulative[:, head : head + 1] - cumulative_t[head : head + 1, :]
            mixing = gram * jnp.exp(jnp.where(inside, gap, -1e30))
            total = total + dot(
                mixing.astype(bf16), jnp.where(keep, scaled, 0.0).astype(bf16), (1, 0)
            )
        z_pair = zx_ref[0, :, cols]
        gated = total * (z_pair * sigmoid(z_pair))
        y_ref[:, cols] = total
        gated_ref[:, cols] = gated
        square = square + gated * gated
    square_ref[...] = as_row(square)


def scan_forward(*values):
    tokens, inner = values[0].shape[1:]
    wide = (tokens, inner)
    shapes = [(wide, f32), (wide, f32), ((1, tokens), f32), (wide, f32), (values[1].shape, bf16)]
    return call(scan_forward_kernel, "scan_forward", shapes, values)


def scan_backward_kernel(
    zx_ref, bc_ref, dt_ref, taps_x_ref, taps_bc_ref, heads_ref, pos_ref, seg_col_ref, seg_row_ref,
    y_ref, xa_ref, ba_ref, up_ref, scale_ref, gain_ref, cross_a, cross_b, cross_c, cross_d, *rest
):
    (
        z_cot_ref, x_cot_ref, bc_cot_ref, dt_cot_ref, taps_x_out, taps_bc_out, heads_out, gain_out
    ) = rest[-8:]
    inner_width = y_ref.shape[1] * 4
    positions = pos_ref[...]
    length = positions.shape[0]
    bc_act = ba_ref[...]
    state = bc_act.shape[1] // 2
    heads = heads_ref[...]
    raw, step, rates, cumulative, cumulative_t, causal, upper = scan_parts(
        dt_ref[...], heads[0:1], heads[1:2]
    )
    inside = causal & (seg_col_ref[...] == seg_row_ref[...])
    gram = dot(bc_act[:, state:], bc_act[:, :state], (1, 1))
    lane = lax.broadcasted_iota(jnp.int32, (length, 128), 1)
    low_half = lane < 64
    scale = scale_ref[...]
    cross = sum_column((cross_a, cross_b, cross_c, cross_d)) / inner_width
    pull = scale * scale * scale * cross
    gram_grad = jnp.zeros((length, length), f32)
    head_lane = lax.broadcasted_iota(jnp.int32, (length, HEAD_PAD), 1)
    head_row = lax.broadcasted_iota(jnp.int32, (HEAD_PAD, length), 0)
    head_one = lax.broadcasted_iota(jnp.int32, (1, HEAD_PAD), 1)
    step_grad = jnp.zeros((length, HEAD_PAD), f32)
    row_sums = jnp.zeros((length, HEAD_PAD), f32)
    col_sums = jnp.zeros((HEAD_PAD, length), f32)
    skip_grad = jnp.zeros((1, HEAD_PAD), f32)
    for pair in range(y_ref.shape[1] // 128):
        cols = slice(pair * 128, pair * 128 + 128)
        first, second = 2 * pair, 2 * pair + 1
        z_pair = zx_ref[0, :, cols]
        y_pair = y_ref[:, cols]
        gate = sigmoid(z_pair)
        silu = z_pair * gate
        gated = y_pair * silu
        up = up_ref[:, cols]
        gain_out[:, cols] = jnp.sum(up * gated * scale, axis=0, keepdims=True)
        gated_grad = scale * (up * gain_ref[:, cols]) - gated * pull
        z_cot_ref[:, cols] = rounded(gated_grad * y_pair * (gate * (1.0 + z_pair * (1.0 - gate))))
        y_grad = gated_grad * silu
        x_pair = xa_ref[:, cols]
        dt_pair = jnp.where(low_half, step[:, first : first + 1], step[:, second : second + 1])
        skip_pair = jnp.where(
            low_half, heads[2:3, first : first + 1], heads[2:3, second : second + 1]
        )
        scaled = (x_pair * dt_pair).astype(bf16)
        scaled_grad = jnp.zeros((length, 128), f32)
        skip_product = y_grad * x_pair
        for head, keep in ((first, low_half), (second, ~low_half)):
            gap = cumulative[:, head : head + 1] - cumulative_t[head : head + 1, :]
            decay = jnp.exp(jnp.where(inside, gap, -1e30))
            mixing = gram * decay
            y_head = jnp.where(keep, y_grad, 0.0).astype(bf16)
            mixing_grad = dot(y_head, scaled, (1, 1))
            scaled_grad = scaled_grad + dot(mixing.astype(bf16), y_head, (0, 0))
            gram_grad = gram_grad + mixing_grad * decay
            moved = mixing_grad * mixing
            row_sums = row_sums + jnp.where(
                head_lane == head, jnp.sum(moved, axis=1, keepdims=True), 0.0
            )
            col_sums = col_sums + jnp.where(
                head_row == head, jnp.sum(moved, axis=0, keepdims=True), 0.0
            )
        step_product = scaled_grad * x_pair
        for head, keep in ((first, low_half), (second, ~low_half)):
            step_grad = step_grad + jnp.where(
                head_lane == head,
                jnp.sum(jnp.where(keep, step_product, 0.0), axis=1, keepdims=True),
                0.0,
            )
            skip_sum = jnp.sum(
                jnp.sum(jnp.where(keep, skip_product, 0.0), axis=0, keepdims=True),
                axis=1,
                keepdims=True,
            )
            skip_grad = skip_grad + jnp.where(head_one == head, skip_sum, 0.0)
        x_grad = scaled_grad * dt_pair + skip_pair * y_grad
        conv_x = conv_values(zx_ref[1, :, cols], taps_x_ref[:, cols], positions)
        gate = sigmoid(conv_x)
        conv_grad = x_grad * (gate * (1.0 + conv_x * (1.0 - gate)))
        total, tap_grads = conv_back(
            conv_grad, zx_ref[1, :, cols], taps_x_ref[:, cols], positions
        )
        x_cot_ref[:, cols] = rounded(total)
        for index, value in enumerate(tap_grads):
            taps_x_out[index : index + 1, cols] = value
    rate_grad = dot(upper, row_sums, (1, 0), highest) - dot(upper, col_sums, (1, 1), highest)
    step_grad = step_grad - rate_grad * jnp.exp(heads[0:1])
    raw_grad = step_grad * sigmoid(raw)
    dt_cot_ref[...] = rounded(raw_grad)
    heads_out[0:1, :] = jnp.sum(rate_grad * rates, axis=0, keepdims=True)
    heads_out[1:2, :] = jnp.sum(raw_grad, axis=0, keepdims=True)
    heads_out[2:3, :] = skip_grad
    gram_low = gram_grad.astype(bf16)
    b_grad = dot(gram_low, bc_act[:, state:], (0, 0))
    c_grad = dot(gram_low, bc_act[:, :state], (1, 0))
    for part, grad in enumerate((b_grad, c_grad)):
        cols = slice(part * state, part * state + state)
        conv = conv_values(bc_ref[:, cols], taps_bc_ref[:, cols], positions)
        gate = sigmoid(conv)
        conv_grad = grad * (gate * (1.0 + conv * (1.0 - gate)))
        total, tap_grads = conv_back(conv_grad, bc_ref[:, cols], taps_bc_ref[:, cols], positions)
        bc_cot_ref[:, cols] = rounded(total)
        for index, value in enumerate(tap_grads):
            taps_bc_out[index : index + 1, cols] = value


def scan_backward(*values, ahead=()):
    zx, bc, dt, taps_x, taps_bc = values[:5]
    tokens, inner = zx.shape[1:]
    shapes = [
        (tokens, inner),
        (tokens, inner),
        bc.shape,
        dt.shape,
        taps_x.shape,
        taps_bc.shape,
        (3, HEAD_PAD),
        (1, inner),
    ]
    shapes = [(shape, f32) for shape in shapes]
    return call(scan_backward_kernel, "scan_backward", shapes, values, ahead)


def turn(values, cosine, sine, low_quarter):
    width = values.shape[1]
    partner = jnp.where(
        low_quarter, pltpu.roll(values, width - HD // 2, 1), pltpu.roll(values, HD // 2, 1)
    )
    return values * cosine + partner * sine


def masked_scores(q_head, kv, allowed):
    scores = dot(q_head, kv, (1, 1)) * HD ** (-0.5)
    return jnp.where(allowed, scores, -1e30)


def softmax(scores):
    exponent = jnp.exp(scores - jnp.max(scores, axis=1, keepdims=True))
    return exponent * (1.0 / jnp.sum(exponent, axis=1, keepdims=True))


def attention_masks(length, seg_col_ref, seg_row_ref):
    row = lax.broadcasted_iota(jnp.int32, (length, length), 0)
    col = lax.broadcasted_iota(jnp.int32, (length, length), 1)
    allowed = (col <= row) & (seg_col_ref[...] == seg_row_ref[...])
    lane = lax.broadcasted_iota(jnp.int32, (length, 2 * HD), 1)
    return allowed, lane < HD, (lane % HD) < HD // 2


def to_low(values, head):
    return values if head == 0 else pltpu.roll(values, HD, 1)


def to_high(values, head):
    return values if head == 1 else pltpu.roll(values, HD, 1)


def attention_forward_kernel(
    head_ref, q_ref, kv_ref, cos_ref, sin_ref, seg_col_ref, seg_row_ref, q_out, kv_out, attn_out
):
    length = q_ref.shape[0]
    allowed, low_half, low_quarter = attention_masks(length, seg_col_ref, seg_row_ref)
    cosine, sine = cos_ref[...], sin_ref[...]
    q_rot = rounded(turn(q_ref[...], cosine, sine, low_quarter))
    first = head_ref[0] == 0
    keys = jnp.where(first, kv_ref[0], pltpu.roll(kv_ref[0], HD, 1))
    kv_in = jnp.where(low_half, keys, jnp.where(first, pltpu.roll(kv_ref[1], HD, 1), kv_ref[1]))
    kv = jnp.where(low_half, turn(kv_in, cosine, sine, low_quarter), kv_in).astype(bf16)
    q_out[...] = q_rot
    kv_out[...] = kv
    parts = []
    for head in range(2):
        q_head = jnp.where(low_half, to_low(q_rot, head), 0.0).astype(bf16)
        probability = softmax(masked_scores(q_head, kv, allowed)).astype(bf16)
        parts.append(dot(probability, kv, (1, 0)))
    attn_out[...] = rounded(jnp.where(low_half, pltpu.roll(parts[0], HD, 1), parts[1]))


def attention_forward(*values):
    shape = values[1].shape
    shapes = [(shape, f32), (shape, bf16), (shape, f32)]
    return call(attention_forward_kernel, "attention_forward", shapes, values)


def attention_backward_kernel(
    head_ref, q_ref, kv_ref, grad_ref, cos_ref, sin_ref, seg_col_ref, seg_row_ref, *rest
):
    q_cot, kv_cot = rest[-2:]
    length = q_ref.shape[0]
    allowed, low_half, low_quarter = attention_masks(length, seg_col_ref, seg_row_ref)
    cosine, sine = cos_ref[...], -sin_ref[...]
    q_rot, kv = q_ref[...], kv_ref[...]
    grad = rounded(grad_ref[...])
    parts = []
    kv_grad = jnp.zeros((length, 2 * HD), f32)
    for head in range(2):
        q_head = jnp.where(low_half, to_low(q_rot, head), 0.0)
        probability = softmax(masked_scores(q_head.astype(bf16), kv, allowed))
        g_head = jnp.where(low_half, 0.0, to_high(grad, head)).astype(bf16)
        prob_grad = dot(g_head, kv, (1, 1))
        inner = jnp.sum(probability * prob_grad, axis=1, keepdims=True)
        score_grad = (probability * (prob_grad - inner)).astype(bf16)
        parts.append(dot(score_grad, kv, (1, 0)) * HD ** (-0.5))
        kv_grad = kv_grad + dot(score_grad, (q_head * HD ** (-0.5)).astype(bf16), (0, 0))
        kv_grad = kv_grad + dot(probability.astype(bf16), g_head, (0, 0))
    q_grad = jnp.where(low_half, parts[0], pltpu.roll(parts[1], HD, 1))
    q_cot[...] = rounded(turn(q_grad, cosine, sine, low_quarter))
    kv_grad = rounded(jnp.where(low_half, turn(kv_grad, cosine, sine, low_quarter), kv_grad))
    turned = pltpu.roll(kv_grad, HD, 1)
    first = head_ref[0] == 0
    kept = low_half == first
    kv_cot[:, : 2 * HD] = jnp.where(kept, jnp.where(first, kv_grad, turned), 0.0)
    kv_cot[:, 2 * HD :] = jnp.where(kept, jnp.where(first, turned, kv_grad), 0.0)


def attention_backward(*values, ahead=()):
    shape = values[1].shape
    shapes = [(shape, f32), ((shape[0], KVH * 2 * HD), f32)]
    return call(attention_backward_kernel, "attention_backward", shapes, values, ahead)


def mix_kernel(
    core_ref, gated_ref, gain_ref, attn_ref, out_w_ref, o_w_ref, sq_a, sq_b, sq_c, sq_d, *rest
):
    mixed_ref, scale_ref, other_ref = rest[-3:]
    inner = gated_ref.shape[1]
    half = gated_ref.shape[0] // 2
    scale = lax.rsqrt(sum_column((sq_a, sq_b, sq_c, sq_d)) / (4 * inner) + epsilon)
    scale_ref[...] = scale
    mixed_ref[:, :inner] = rounded(gated_ref[...] * scale * gain_ref[...])
    mixed_ref[:, inner:] = attn_ref[...]
    other_ref[...] = mix_product(mixed_ref, out_w_ref, o_w_ref, half_rows(1 - core_ref[0], half))


def mix_product(mixed_ref, out_w_ref, o_w_ref, span):
    inner = out_w_ref.shape[0]
    part = mixed_ref[span, :].astype(bf16)
    return dot(part[:, :inner], out_w_ref[...], (1, 0)) + dot(part[:, inner:], o_w_ref[...], (1, 0))


def mix_mine_kernel(core_ref, mixed_ref, out_w_ref, o_w_ref, got_ref, mine_ref):
    half = got_ref.shape[0]
    span = half_rows(core_ref[0], half)
    mine_ref[...] = mix_product(mixed_ref, out_w_ref, o_w_ref, span) + got_ref[...]


def feed_product(gate_cot_ref, up_cot_ref, gu_ref, span):
    gate_part = gate_cot_ref[span, :].astype(bf16)
    up_part = up_cot_ref[span, :].astype(bf16)
    return dot(gate_part, gu_ref[0], (1, 1)) + dot(up_part, gu_ref[1], (1, 1))


def feed_kernel(core_ref, mine_ref, got_ref, in_ref, gain_ref, act_grad_ref, gu_ref, *rest):
    resid_ref, scale_ref, normed_ref, act_ref, gate_cot_ref, up_cot_ref, other_ref = rest[-7:]
    core = core_ref[0]
    half = mine_ref.shape[0]
    for which, ref in ((core, mine_ref), (1 - core, got_ref)):
        span = half_rows(which, half)
        resid_ref[span, :] = in_ref[span, :].astype(f32) + ref[...]
    resid = resid_ref[...]
    scale = rms_scale(resid)
    scale_ref[...] = scale
    normed_ref[...] = (resid * scale * gain_ref[...]).astype(bf16)
    normed = normed_ref[...]
    hidden = gu_ref.shape[2]
    for start in range(0, hidden, 256):
        cols = slice(start, start + 256)
        gate = dot(normed, gu_ref[0, :, cols], (1, 0))
        up = dot(normed, gu_ref[1, :, cols], (1, 0))
        slope = sigmoid(gate)
        silu = gate * slope
        act_ref[:, cols] = rounded(silu * up)
        act_grad = act_grad_ref[:, cols]
        gate_cot_ref[:, cols] = rounded(act_grad * up * slope * (1.0 + gate * (1.0 - slope)))
        up_cot_ref[:, cols] = rounded(act_grad * silu)
    other_ref[...] = feed_product(gate_cot_ref, up_cot_ref, gu_ref, half_rows(1 - core, half))


def feed_mine_kernel(core_ref, gate_cot_ref, up_cot_ref, gu_ref, got_ref, *rest):
    span = half_rows(core_ref[0], got_ref.shape[0])
    rest[-1][...] = feed_product(gate_cot_ref, up_cot_ref, gu_ref, span) + got_ref[...]


def mix_back_kernel(
    core_ref, mine_ref, got_ref, resid_ref, scale_ref, gain_ref, out_grad_ref, out_w_ref, o_w_ref,
    gated_ref, gated_gain_ref, *rest,
):
    grad_ref, mix_ref, gain_grad_ref, up_ref, attn_grad_ref, cross_ref = rest[-6:]
    core = core_ref[0]
    half = mine_ref.shape[0]
    for which, ref in ((core, mine_ref), (1 - core, got_ref)):
        grad_ref[half_rows(which, half), :] = ref[...]
    normed_grad = grad_ref[...]
    resid = resid_ref[...]
    scale = scale_ref[...]
    gain_grad_ref[...] = jnp.sum(normed_grad * resid * scale, axis=0, keepdims=True)
    weighted = normed_grad * gain_ref[...]
    mean = jnp.mean(weighted * resid, axis=1, keepdims=True)
    resid_grad = (
        out_grad_ref[...].astype(f32) + scale * weighted - resid * (scale * scale * scale * mean)
    )
    grad_ref[...] = resid_grad
    mix = resid_grad.astype(bf16)
    mix_ref[...] = mix
    up = dot(mix, out_w_ref[...], (1, 1))
    up_ref[...] = up
    attn_grad_ref[...] = dot(mix, o_w_ref[...], (1, 1))
    cross_ref[...] = as_row(up * gated_gain_ref[...] * gated_ref[...])


def call_dense(kernel, name, shapes, core, values, ahead=(), scratch=()):
    scratch = [(shape, f32) for shape in scratch]
    return call(kernel, name, shapes, (core, *values), ahead, scratch)


def chunks(values):
    return [
        (value, row, start)
        for value in values
        for row in range(value.shape[0])
        for start in range(0, value.shape[1], 128)
    ]


def pick(index, blocks):
    total = blocks[0]
    for place in range(1, len(blocks)):
        total = jnp.where(index == place, blocks[place], total)
    return total


def shared_blocks(bc_ref, kv_ref):
    return [ref[:, at : at + 128] for ref in (bc_ref, kv_ref) for at in (0, 128)]


def post_kernel(core_ref, me_ref, grad_ref, in_ref, taps_ref, bc_ref, kv_ref, *rest):
    mine_ref, other_ref, near_ref, state_ref = rest[-4:]
    half = mine_ref.shape[0]
    tokens = 2 * half
    mine_ref[...] = grad_ref[half_rows(core_ref[0], half), :]
    other_ref[...] = grad_ref[half_rows(1 - core_ref[0], half), :]
    inputs = in_ref[...].astype(f32)
    gain = jnp.sum(grad_ref[...] * inputs * rms_scale(inputs), axis=0, keepdims=True)
    state_ref[...] = jnp.zeros_like(state_ref)
    for at, (value, row, start) in enumerate(chunks((gain, taps_ref[...]))):
        state_ref[at : at + 1, :] = value[row : row + 1, start : start + 128]
    blocks = shared_blocks(bc_ref, kv_ref)
    near_ref[:tokens, :] = pick(me_ref[0] ^ 1, blocks)
    near_ref[tokens : 2 * tokens, :] = pick(me_ref[0] ^ 3, blocks)
    near_ref[2 * tokens :, :] = state_ref[...]


def share_kernel(core_ref, me_ref, near_ref, bc_ref, kv_ref, state_ref, far_ref):
    tokens = bc_ref.shape[0]
    blocks = shared_blocks(bc_ref, kv_ref)
    far_ref[:tokens, :] = pick(me_ref[0] ^ 2, blocks) + near_ref[tokens : 2 * tokens, :]
    far_ref[tokens:, :] = state_ref[...] + near_ref[2 * tokens :, :]


def few_kernel(
    core_ref, me_ref, near_ref, far_own_ref, far_ref, bc_ref, kv_ref, q_ref, dt_ref, gain_two_ref,
    taps_ref, gain_ref, heads_ref, *rest
):
    few_ref = rest[-1]
    tokens = bc_ref.shape[0]
    blocks = shared_blocks(bc_ref, kv_ref)
    few_ref[:tokens, :128] = q_ref[...]
    few_ref[:tokens, 128:256] = (
        pick(me_ref[0], blocks) + near_ref[:tokens, :] + far_ref[:tokens, :]
    )
    few_ref[:tokens, 256:] = dt_ref[...]
    state = far_own_ref[tokens:, :] + far_ref[tokens:, :]
    used = STATE_ROWS
    few_ref[tokens:, :] = jnp.zeros((few_ref.shape[0] - tokens, few_ref.shape[1]), f32)
    values = (state[:used], gain_two_ref[...], taps_ref[...], gain_ref[...], heads_ref[...])
    for at, (value, row, start) in enumerate(chunks(values)):
        place = tokens + at // 3
        cols = slice(at % 3 * 128, at % 3 * 128 + 128)
        few_ref[place : place + 1, cols] = value[row : row + 1, start : start + 128]


def unpack_kernel(core_ref, few_ref, own_ref, *refs):
    rows_out = own_ref.shape[0]
    own_ref[...] = few_ref[:rows_out, 128:256]
    for at, (ref, row, start) in enumerate(chunks(refs)):
        place = rows_out + at // 3
        cols = slice(at % 3 * 128, at % 3 * 128 + 128)
        ref[row : row + 1, start : start + 128] = few_ref[place : place + 1, cols]


def assemble_kernel(core_ref, me_ref, own_ref, near_ref, far_ref, far_near_ref, bc_ref, *kv_refs):
    blocks = (own_ref[...], near_ref[...], far_ref[...], far_near_ref[...])
    for place in range(4):
        value = pick(me_ref[0] ^ place, blocks)
        if place < 2:
            bc_ref[:, place * 128 : place * 128 + 128] = value
        else:
            kv_refs[place - 2][...] = value


def input_grad_kernel(core_ref, mine_ref, got_ref, grad_ref, in_ref, gain_ref, out_ref, full_ref):
    half = mine_ref.shape[0]
    full_ref[half_rows(core_ref[0], half), :] = mine_ref[...]
    full_ref[half_rows(1 - core_ref[0], half), :] = got_ref[...]
    inputs = in_ref[...].astype(f32)
    scale = rms_scale(inputs)
    weighted = full_ref[...] * gain_ref[...]
    mean = jnp.mean(weighted * inputs, axis=1, keepdims=True)
    total = grad_ref[...] + scale * weighted - inputs * (scale * scale * scale * mean)
    out_ref[...] = total.astype(bf16)


def layer_out_kernel(core_ref, mine_ref, got_ref, resid_ref, out_ref, full_ref):
    half = mine_ref.shape[0]
    full_ref[half_rows(core_ref[0], half), :] = mine_ref[...]
    full_ref[half_rows(1 - core_ref[0], half), :] = got_ref[...]
    out_ref[...] = (resid_ref[...] + full_ref[...]).astype(bf16)


def rotary_tables(positions):
    half = HD // 2
    frequency = rope_base ** (-jnp.arange(half, dtype=f32) / half)
    angles = positions.astype(f32)[:, None] * frequency[None, :]
    cosine, sine = jnp.cos(angles), jnp.sin(angles)
    return (
        jnp.concatenate([cosine] * 4, axis=1),
        jnp.concatenate([-sine, sine, -sine, sine], axis=1),
    )


def on_device(
    hidden,
    positions,
    out_grad,
    norm_one,
    zx_weight,
    bc_weight,
    dt_weight,
    conv_inner,
    conv_state,
    decay_log,
    dt_bias,
    skip_gain,
    gated_gain,
    out_weight,
    q_weight,
    kv_weight,
    o_weight,
    norm_two,
    gu_weight,
    down_weight,
):
    tokens, model = hidden.shape
    head_count = dt_weight.shape[1]
    inner_cols = conv_inner.shape[1]
    hidden_cols = gu_weight.shape[2]
    query_cols = q_weight.shape[1]
    segment = jnp.cumsum((positions == 0).astype(jnp.int32), dtype=jnp.int32)
    seg_col, seg_row, pos_col = segment[:, None], segment[None, :], positions[:, None]
    cosine, sine = rotary_tables(positions)
    head_pad = ((0, 0), (0, HEAD_PAD - head_count))
    heads = jnp.pad(jnp.stack([decay_log, dt_bias, skip_gain]), head_pad)
    dt_wide = jnp.pad(dt_weight, head_pad)

    core = lax.axis_index("tensor").astype(jnp.int32) % 2
    core_arg = core.reshape(1)
    kv_head = (lax.axis_index("tensor") * (query_cols // HD) // (QH // KVH)).astype(jnp.int32)
    kv_head = kv_head.reshape(1)
    half = tokens // 2
    half_model = model // 2
    wide = (tokens, model)
    half_wide = (half, model)

    inputs = hidden.astype(f32)
    scale_one = rms_scale(inputs)
    normed = (inputs * scale_one * norm_one).astype(bf16)
    own_normed, normed_sent = arrange(1, normed)
    normed_pair = (own_normed, *swap_shared(normed_sent, 1))
    own_out, out_sent = arrange(2, out_grad)
    out_pair = (own_out, *swap_shared(out_sent, 2))

    proj_zx = jnp.einsum("td,dkc->ktc", normed, zx_weight, preferred_element_type=f32)
    proj_bc = dot(normed, bc_weight, (1, 0))
    proj_dt = dot(normed, dt_wide, (1, 0))
    scan_args = (
        proj_zx, proj_bc, proj_dt, conv_inner, conv_state, heads, pos_col, seg_col, seg_row
    )
    y, gated, square, x_act, bc_act = scan_forward(*scan_args)
    squares = spread_tensor(square)

    query = dot(normed, q_weight, (1, 0))
    key_value = jnp.einsum("td,dkc->ktc", normed, kv_weight, preferred_element_type=f32)
    q_rot, kv_rot, attn = attention_forward(
        kv_head, query, key_value, cosine, sine, seg_col, seg_row
    )
    act_grad = dot(out_grad, down_weight, (1, 1))
    gu_split = gu_weight.transpose(1, 0, 2)

    gain_row = gated_gain[None, :]
    mixed, gate_scale, other = call_dense(
        mix_kernel,
        "mix",
        [((tokens, inner_cols + query_cols), f32), ((tokens, 1), f32), (half_wide, f32)],
        core_arg,
        (gated, gain_row, attn, out_weight, o_weight, *squares),
        (normed_pair[1],),
    )
    mixed_got = swap(mixed, "dp", 1)
    mixed_pair = (mixed, mixed_got)
    (mine,) = call_dense(
        mix_mine_kernel,
        "mix_mine",
        [(half_wide, f32)],
        core_arg,
        (mixed, out_weight, o_weight, swap(other, "tensor", 1)),
    )
    resid, scale_two, normed_two, act, gate_cot, up_cot, other = call_dense(
        feed_kernel,
        "feed",
        [
            (wide, f32),
            ((tokens, 1), f32),
            (wide, bf16),
            ((tokens, hidden_cols), f32),
            ((tokens, hidden_cols), f32),
            ((tokens, hidden_cols), f32),
            (half_wide, f32),
        ],
        core_arg,
        (
            *tensor_halves(mine, (out_pair[1], mixed_got, act_grad, gu_split)),
            hidden,
            norm_two[None, :],
            act_grad,
            gu_split,
        ),
    )
    (mine,) = call_dense(
        feed_mine_kernel,
        "feed_mine",
        [(half_wide, f32)],
        core_arg,
        (gate_cot, up_cot, gu_split, swap(other, "tensor", 1)),
    )
    act_got = swap(act, "dp", 2)
    own_up, sent_up = arrange(1, normed_two)
    two_up = swap_shared(sent_up, 1)
    own_gate, sent_gate = arrange(2, normed_two)
    two_gate = swap_shared(sent_gate, 2)
    up_got = swap(up_cot, "dp", 1)
    gate_got = swap(gate_cot, "dp", 2)
    down_stages = halving(out_pair, (act, act_got), False, 2)
    gate_stages = halving((own_gate, *two_gate), (gate_cot, gate_got), True, 2)
    up_stages = halving((own_up, *two_up), (up_cot, up_got), True)
    for stages in (down_stages, gate_stages, up_stages):
        next(stages)
    halves = tensor_halves(mine, (act_got, *two_up, *two_gate, up_got))
    up_first, up_one = up_stages.send((halves[0],))
    resid_grad, mix_grad, norm_two_grad, up, attn_grad, cross = call_dense(
        mix_back_kernel,
        "mix_back",
        [
            (wide, f32),
            (wide, bf16),
            ((1, model), f32),
            ((tokens, inner_cols), f32),
            ((tokens, query_cols), f32),
            ((1, tokens), f32),
        ],
        core_arg,
        (
            *halves,
            resid,
            scale_two,
            norm_two[None, :],
            out_grad,
            out_weight,
            o_weight,
            gated,
            gain_row,
        ),
        (up_first,),
    )
    own_mix, sent_mix = arrange(1, mix_grad)
    mix_pair = (own_mix, *swap_shared(sent_mix, 1))
    crosses = spread_tensor(cross)
    last, gate_one = gate_stages.send((up,))
    q_cot, kv_cot = attention_backward(
        kv_head, q_rot, kv_rot, attn_grad, cosine, sine, seg_col, seg_row, ahead=(last, own_mix)
    )

    mix_stages = halving(mix_pair, mixed_pair, False)
    next(mix_stages)
    act_b = act.astype(bf16)
    mlp_other = dot(rows(act_b, (1 - core) * half, half), down_weight, (1, 0))
    mlp_mine = dot(rows(act_b, core * half, half), down_weight, (1, 0)) + swap(
        mlp_other, "tensor", 1
    )

    z_cot, x_cot, bc_cot, dt_cot, taps_x_grad, taps_bc_grad, heads_grad, gain_grad = scan_backward(
        *scan_args, y, x_act, bc_act, up, gate_scale, gain_row, *crosses, ahead=(q_cot,)
    )

    zx_cot = jnp.stack([z_cot, x_cot], axis=1).astype(bf16)
    normed_grad = (
        jnp.einsum("tkc,dkc->td", zx_cot, zx_weight, preferred_element_type=f32)
        + dot(bc_cot.astype(bf16), bc_weight, (1, 1))
        + dot(dt_cot.astype(bf16), dt_wide, (1, 1))
        + dot(q_cot.astype(bf16), q_weight, (1, 1))
        + jnp.einsum(
            "tkc,dkc->td",
            kv_cot.astype(bf16).reshape(tokens, 2, KVH * HD),
            kv_weight,
            preferred_element_type=f32,
        )
    )
    me_arg = lax.axis_index("tensor").astype(jnp.int32).reshape(1)
    normed_mine, normed_other, near, state_part = call_dense(
        post_kernel,
        "post",
        [
            (half_wide, f32),
            (half_wide, f32),
            ((2 * tokens + STATE_PAD, 128), f32),
            ((STATE_PAD, 128), f32),
        ],
        core_arg,
        (me_arg, normed_grad, hidden, taps_bc_grad, bc_cot, kv_cot),
        (mix_pair[1],),
    )
    zx_own = jnp.concatenate([z_cot, x_cot], axis=1)
    zx_got = swap(zx_own, "dp", 1)
    zx_stages = halving(normed_pair, (zx_own, zx_got), True)
    near = swap(near, "tensor", 1)
    (far_own,) = call_dense(
        share_kernel,
        "share",
        [((tokens + STATE_PAD, 128), f32)],
        core_arg,
        (me_arg, near, bc_cot, kv_cot, state_part),
    )
    far = swap(far_own, "tensor", 2)
    (few,) = call_dense(
        few_kernel,
        "few",
        [((tokens + SMALL_ROWS, 384), f32)],
        core_arg,
        (
            me_arg, near, far_own, far, bc_cot, kv_cot, q_cot, dt_cot, norm_two_grad, taps_x_grad,
            gain_grad, heads_grad,
        ),
    )
    few_got = swap(few, "dp", 1)
    few_stages = halving(normed_pair, (few, few_got), True)
    next(zx_stages)
    next(few_stages)
    normed_mine = normed_mine + swap(normed_other, "tensor", 1)

    gots = {"up": [up_one], "gate": [gate_one]}
    totals = {}
    stage_list = {
        "down": down_stages,
        "gate": gate_stages,
        "up": up_stages,
        "mix": mix_stages,
        "zx": zx_stages,
        "few": few_stages,
    }

    def advance(name, *ahead):
        value, got = stage_list[name].send(ahead)
        gots.setdefault(name, []).append(got)
        totals[name] = value
        return value

    last = advance("up", x_cot)
    last = advance("mix", last, far_own)
    last = advance("gate", last, zx_got)
    last = advance("zx", last)
    last = advance("mix", last, few)
    last = advance("few", last)
    last = advance("down", last)
    last = advance("up", last)
    last = advance("gate", last)
    last = advance("zx", last)
    last = advance("few", last)
    normed_mine, normed_other = tensor_halves(normed_mine, (last,))
    last = normed_mine
    last = advance("down", last)
    last = advance("mix", last)
    last = advance("zx", last)
    last = advance("few", last)
    last = advance("down", last)
    (input_grad,) = call_dense(
        input_grad_kernel,
        "input_grad",
        [(wide, bf16)],
        core_arg,
        (normed_mine, normed_other, resid_grad, hidden, norm_one[None, :]),
        scratch=(wide,),
    )
    (layer_out,) = call_dense(
        layer_out_kernel,
        "layer_out",
        [(wide, bf16)],
        core_arg,
        (*tensor_halves(mlp_mine, (x_cot,)), resid),
        scratch=(wide,),
    )
    for name, stages in stage_list.items():
        for value, _ in stages:
            totals[name] = value
    down_shard, mixed_shard = totals["down"], totals["mix"]
    out_shard, o_shard = mixed_shard[:inner_cols], mixed_shard[inner_cols:]
    gu_shard = jnp.stack([totals["gate"], totals["up"]], axis=1)
    zx_shard = totals["zx"].reshape(-1, 2, inner_cols)
    few_shard = totals["few"]
    shard_rows = model // lax.axis_size("dp")
    q_shard = few_shard[:shard_rows, :query_cols]
    dt_shard = few_shard[:shard_rows, 256 : 256 + head_count]
    own, norm_one_grad, state_grad, norm_two_grad, inner_grad, gain_grad, heads_grad = call_dense(
        unpack_kernel,
        "unpack",
        [
            ((shard_rows, 128), f32),
            ((1, model), f32),
            (conv_state.shape, f32),
            ((1, model), f32),
            (conv_inner.shape, f32),
            ((1, inner_cols), f32),
            ((3, HEAD_PAD), f32),
        ],
        core_arg,
        (few_shard,),
    )
    head_sums = heads_grad[:, :head_count]
    near = swap(own, "tensor", 1)
    bc_shard, *kv_parts = call_dense(
        assemble_kernel,
        "assemble",
        [((shard_rows, 256), f32), ((shard_rows, 128), f32), ((shard_rows, 128), f32)],
        core_arg,
        (me_arg, own, near, swap(own, "tensor", 2), swap(own, "tensor", 3)),
    )
    kv_shard = jnp.stack(kv_parts, axis=1)
    return (
        layer_out,
        input_grad,
        norm_one_grad.reshape(-1),
        zx_shard,
        bc_shard,
        dt_shard,
        inner_grad,
        state_grad,
        head_sums[0],
        head_sums[1],
        head_sums[2],
        gain_grad.reshape(-1),
        out_shard,
        q_shard,
        kv_shard,
        o_shard,
        norm_two_grad.reshape(-1),
        gu_shard,
        down_shard,
    )


def solution(mesh):
    placed = (
        P("dp", None),
        P("dp"),
        P("dp", None),
        P(),
        P(None, None, "tensor"),
        P(),
        P(None, "tensor"),
        P(None, "tensor"),
        P(),
        P("tensor"),
        P("tensor"),
        P("tensor"),
        P("tensor"),
        P("tensor", None),
        P(None, "tensor"),
        P(),
        P("tensor", None),
        P(),
        P(None, None, "tensor"),
        P("tensor", None),
    )
    return jax.shard_map(
        on_device,
        mesh=mesh,
        in_specs=placed,
        out_specs=(
            P("dp", None),
            P("dp", None),
            P(),
            P("dp", None, "tensor"),
            P("dp", None),
            P("dp", "tensor"),
            P(None, "tensor"),
            P(),
            P("tensor"),
            P("tensor"),
            P("tensor"),
            P("tensor"),
            P("tensor", "dp"),
            P("dp", "tensor"),
            P("dp", None, None),
            P("tensor", "dp"),
            P(),
            P("dp", None, "tensor"),
            P("tensor", "dp"),
        ),
        check_vma=False,
    )
```

profile of v0, /device:TPU:0, one launch (start us, length us, event | category | flops | bytes accessed | tf_op | source)
XLA Modules:
  0.0 224.7 jit_solution(3074262431212666400)
XLA Ops:
  7.1 1.9 scan_forward.1
  12.0 2.4 %collective-permute-start.2 = (f32[1,256]{1,0:T(1,128)S(1)}, f32[1,256]{1,0:T(1,128)}, u32[]{:S(2)}, u32[]{:S(2)}) collective-permute-start(f32[1,256]{1,0:T(1,128)S(1)} %get-tuple-element.79.sq_a), channel_id=1, source_target_pairs={{0,3},{1,2},{2,1},{3,0},{4,7},{5,6},{6,5},{7,4},{8,11},{9,10},{10,... | collective-permute-start | bytes 3080 | tf_op jit(solution)/shard_map/ppermute | solution.py:80
  16.5 1.7 collective-permute-start.3
  34.2 5.6 %collective-permute-done.6.rest_0_.refs_1_ = f32[128,512]{1,0:T(8,128)S(1)} collective-permute-done((f32[128,512]{1,0:T(8,128)S(1)}, f32[128,512]{1,0:T(8,128)S(1)}, u32[]{:S(2)}, u32[]{:S(2)}) %collective-permute-start.6) | collective-permute-done | bytes 262176 | tf_op jit(solution)/shard_map/ppermute | solution.py:80
  39.8 1.7 collective-permute-done.7.rest_1_.refs_4_
  41.6 2.0 collective-permute-done.5.right_ref
  43.7 1.9 collective-permute-done.8.got_ref
  45.6 1.9 feed.1
  55.2 2.7 %feed_mine.1.left_ref = f32[128,1024]{1,0:T(8,128)} custom-call(s32[1]{0:T(128)} %bitcast.core_ref, f32[256,512]{1,0:T(8,128)S(1)} %get-tuple-element.88.gate_cot_ref.refs_3_, f32[256,512]{1,0:T(8,128)} %get-tuple-element.89.up_cot_ref.refs_3_, bf16[2,1024,512]{2,1,0:T(8,128)(2,1)S(1)} %bitcast.66, f32[128,1024]{1,0:T(8,128)S(1)} %collective-permute-done.11.got_ref), custom_call_target="tpu_custom_call" | custom-call | flops 3000000000 | bytes 1000000 | tf_op jit(solution)/shard_map/feed_mine/pallas_call | solution.py:64
  59.5 2.6 %collective-permute-done.16.rest_3_.refs_1_ = f32[128,512]{1,0:T(8,128)} collective-permute-done((f32[128,512]{1,0:T(8,128)}, f32[128,512]{1,0:T(8,128)}, u32[]{:S(2)}, u32[]{:S(2)}) %collective-permute-start.16) | collective-permute-done | bytes 262176 | tf_op jit(solution)/shard_map/ppermute | solution.py:80
  62.1 2.3 %fusion.29 = f32[128,1024]{1,0:T(8,128)} fusion(bf16[512,1024]{1,0:T(8,128)(2,1)} %param.39, bf16[256,512]{1,0:T(8,128)(2,1)S(1)} %convert_element_type.33, s32[]{:T(128)S(6)} %select_n.66), kind=kOutput, calls=%fused_computation.42 | convolution fusion | flops 134217728 | bytes 1703940 | tf_op jit(solution)/shard_map/dot_general | solution.py:28
  65.7 6.8 %collective-permute-done.13.rest_0_.refs_4_ = f32[256,512]{1,0:T(8,128)} collective-permute-done((f32[256,512]{1,0:T(8,128)S(1)}, f32[256,512]{1,0:T(8,128)}, u32[]{:S(2)}, u32[]{:S(2)}) %collective-permute-start.13) | collective-permute-done | bytes 524320 | tf_op jit(solution)/shard_map/ppermute | solution.py:80
  79.5 1.8 pair_product.18.rest_0_
  81.5 1.7 mix_back.1
  89.5 2.3 %collective-permute-done.22.cross_d = f32[1,256]{1,0:T(1,128)S(1)} collective-permute-done((f32[1,256]{1,0:T(1,128)S(1)}, f32[1,256]{1,0:T(1,128)S(1)}, u32[]{:S(2)}, u32[]{:S(2)}) %collective-permute-start.22) | collective-permute-done | bytes 1056 | tf_op jit(solution)/shard_map/ppermute | solution.py:80
  94.4 3.9 %scan_backward.1 = (f32[256,384]{1,0:T(8,128)S(1)}, f32[256,384]{1,0:T(8,128)S(1)}, f32[256,256]{1,0:T(8,128)S(1)}, f32[256,128]{1,0:T(8,128)S(1)}, f32[5,384]{1...) custom-call(f32[2,256,384]{2,1,0:T(8,128)S(1)} %copy-done.39, ...), custom_call_target="tpu_custom_call" | custom-call | flops 3000000000 | bytes 1000000 | tf_op jit(solution)/shard_map/scan_backward/pallas_call | solution.py:64
  101.7 4.5 %collective-permute-done.33.refs_5_ = f32[256,512]{1,0:T(8,128)S(1)} collective-permute-done((f32[256,512]{1,0:T(8,128)S(1)}, f32[256,512]{1,0:T(8,128)S(1)}, u32[]{:S(2)}, u32[]{:S(2)}) %collective-permute-start.33) | collective-permute-done | bytes 524320 | tf_op jit(solution)/shard_map/ppermute | solution.py:80
  108.4 4.4 %collective-permute-done.25.rest_0_.refs_1_ = f32[128,512]{1,0:T(8,128)S(1)} collective-permute-done((f32[128,512]{1,0:T(8,128)S(1)}, f32[128,512]{1,0:T(8,128)S(1)}, u32[]{:S(2)}, u32[]{:S(2)}) %collective-permute-start.25) | collective-permute-done | bytes 262176 | tf_op jit(solution)/shard_map/ppermute | solution.py:80
  118.0 4.0 %collective-permute-done.30.far_ref = f32[280,128]{1,0:T(8,128)S(1)} collective-permute-done((f32[280,128]{1,0:T(8,128)S(1)}, f32[280,128]{1,0:T(8,128)S(1)}, u32[]{:S(2)}, u32[]{:S(2)}) %collective-permute-start.30) | collective-permute-done | bytes 143392 | tf_op jit(solution)/shard_map/ppermute | solution.py:80
  122.1 2.7 %collective-permute-start.40 = (f32[128,512]{1,0:T(8,128)S(1)}, f32[128,512]{1,0:T(8,128)S(1)}, u32[]{:S(2)}, u32[]{:S(2)}) collective-permute-start(f32[128,512]{1,0:T(8,128)S(1)} %pair_product.20.refs_5_), channel_id=1, source_target_pairs={{0,16},{4,20},{8,24},{12,28},{16,0},{20,4},{24,8},{28,12},{1,17},{... | collective-permute-start | bytes 786440 | tf_op jit(solution)/shard_map/ppermute | solution.py:80
  126.5 2.4 %collective-permute-done.35.refs_7_.refs_4_ = f32[256,768]{1,0:T(8,128)S(1)} collective-permute-done((f32[256,768]{1,0:T(8,128)S(1)}, f32[256,768]{1,0:T(8,128)S(1)}, u32[]{:S(2)}, u32[]{:S(2)}) %collective-permute-start.35) | collective-permute-done | bytes 786464 | tf_op jit(solution)/shard_map/ppermute | solution.py:80
  132.8 10.9 %collective-permute-done.34.refs_5_ = f32[512,256]{1,0:T(8,128)S(1)} collective-permute-done((f32[512,256]{1,0:T(8,128)S(1)}, f32[512,256]{1,0:T(8,128)S(1)}, u32[]{:S(2)}, u32[]{:S(2)}) %collective-permute-start.34) | collective-permute-done | bytes 524320 | tf_op jit(solution)/shard_map/ppermute | solution.py:80
  145.0 1.9 collective-permute-start.38
  152.7 6.2 %collective-permute-done.39.refs_6_ = f32[128,512]{1,0:T(8,128)S(1)} collective-permute-done((f32[128,512]{1,0:T(8,128)S(1)}, f32[128,512]{1,0:T(8,128)S(1)}, u32[]{:S(2)}, u32[]{:S(2)}) %collective-permute-start.39) | collective-permute-done | bytes 262176 | tf_op jit(solution)/shard_map/ppermute | solution.py:80
  162.0 13.7 %collective-permute-done.38.refs_5_ = f32[256,768]{1,0:T(8,128)S(1)} collective-permute-done((f32[256,768]{1,0:T(8,128)S(1)}, f32[256,768]{1,0:T(8,128)S(1)}, u32[]{:S(2)}, u32[]{:S(2)}) %collective-permute-start.38) | collective-permute-done | bytes 786464 | tf_op jit(solution)/shard_map/ppermute | solution.py:80
  176.1 1.7 collective-permute-start.44
  177.8 12.8 %collective-permute-done.37.refs_5_ = f32[272,384]{1,0:T(8,128)S(1)} collective-permute-done((f32[272,384]{1,0:T(8,128)S(1)}, f32[272,384]{1,0:T(8,128)S(1)}, u32[]{:S(2)}, u32[]{:S(2)}) %collective-permute-start.37) | collective-permute-done | bytes 417824 | tf_op jit(solution)/shard_map/ppermute | solution.py:80
  194.2 2.9 %collective-permute-start.50 = (f32[512,128]{1,0:T(8,128)S(1)}, f32[512,128]{1,0:T(8,128)S(1)}, u32[]{:S(2)}, u32[]{:S(2)}) collective-permute-start(f32[512,128]{1,0:T(8,128)S(1)} %pair_product.31.refs_7_), channel_id=1, source_target_pairs={{0,16},{4,20},{8,24},{12,28},{16,0},{20,4},{24,8},{28,12},{1,17},{... | collective-permute-start | bytes 786440 | tf_op jit(solution)/shard_map/ppermute | solution.py:80
  197.1 9.2 %collective-permute-done.44.refs_6_ = f32[128,768]{1,0:T(8,128)S(1)} collective-permute-done((f32[128,768]{1,0:T(8,128)S(1)}, f32[128,768]{1,0:T(8,128)S(1)}, u32[]{:S(2)}, u32[]{:S(2)}) %collective-permute-start.44) | collective-permute-done | bytes 393248 | tf_op jit(solution)/shard_map/ppermute | solution.py:80
  206.7 4.4 %collective-permute-done.43.refs_6_ = f32[144,384]{1,0:T(8,128)S(1)} collective-permute-done((f32[144,384]{1,0:T(8,128)S(1)}, f32[144,384]{1,0:T(8,128)S(1)}, u32[]{:S(2)}, u32[]{:S(2)}) %collective-permute-start.43) | collective-permute-done | bytes 221216 | tf_op jit(solution)/shard_map/ppermute | solution.py:80
  215.2 2.1 pair_product.35
  222.2 2.4 %input_grad.1 = bf16[256,1024]{1,0:T(8,128)(2,1)} custom-call(s32[1]{0:T(128)} %bitcast.core_ref, f32[128,1024]{1,0:T(8,128)S(1)} %add_halves.7.mine_ref.refs_6_, f32[128,1024]{1,0:T(8,128)} %collective-permute-done.42.got_ref, f32[256,1024]{1,0:T(8,128)S(1)} %copy-done.41, bf16[256,1024]{1,0:T(8,128)(2,1)S(1)} %copy-done.2, f32[1,1024]{1,0:T(1,128)S(1)} %bitcast.71), custom_call_target="tpu_custom_call" | custom-call | flops 3000000000 | bytes 1000000 | tf_op jit(solution)/shard_map/input_grad/pallas_call | solution.py:64
  (333 shorter events, 93.4 us)
Async XLA Ops:
  12.0 13.0 %collective-permute-start.2 = (f32[1,256]{1,0:T(1,128)S(1)}, f32[1,256]{1,0:T(1,128)}, u32[]{:S(2)}, u32[]{:S(2)}) collective-permute-start(f32[1,256]{1,0:T(1,128)S(1)} %get-tuple-element.79.sq_a), channel_id=1, source_target_pairs={{0,3},{1,2},{2,1},{3,0},{4,7},{5,6},{6,5},{7,4},{8,11},{9,10},{10,... | collective-permute-start | bytes 3080 | tf_op jit(solution)/shard_map/ppermute | solution.py:80
  14.4 10.6 %collective-permute-start.1 = (f32[1,256]{1,0:T(1,128)S(1)}, f32[1,256]{1,0:T(1,128)}, u32[]{:S(2)}, u32[]{:S(2)}) collective-permute-start(f32[1,256]{1,0:T(1,128)S(1)} %get-tuple-element.79.sq_a), channel_id=1, source_target_pairs={{0,2},{1,3},{2,0},{3,1},{4,6},{5,7},{6,4},{7,5},{8,10},{9,11},{10,... | collective-permute-start | bytes 3080 | tf_op jit(solution)/shard_map/ppermute | solution.py:80
  15.0 10.0 %collective-permute-start = (f32[1,256]{1,0:T(1,128)S(1)}, f32[1,256]{1,0:T(1,128)}, u32[]{:S(2)}, u32[]{:S(2)}) collective-permute-start(f32[1,256]{1,0:T(1,128)S(1)} %get-tuple-element.79.sq_a), channel_id=1, source_target_pairs={{0,1},{1,0},{2,3},{3,2},{4,5},{5,4},{6,7},{7,6},{8,9},{9,8},{10,11... | collective-permute-start | bytes 3080 | tf_op jit(solution)/shard_map/ppermute | solution.py:80
  27.2 14.3 %collective-permute-start.7 = (f32[256,512]{1,0:T(8,128)S(1)}, f32[256,512]{1,0:T(8,128)S(1)}, u32[]{:S(2)}, u32[]{:S(2)}) collective-permute-start(f32[256,512]{1,0:T(8,128)S(1)} %get-tuple-element.81.mixed_ref.refs_3_), channel_id=1, source_target_pairs={{0,4},{4,0},{8,12},{12,8},{16,20},{20,16},{24,28},{28,24},{1,5},{5... | collective-permute-start | bytes 1572872 | tf_op jit(solution)/shard_map/ppermute | solution.py:80
  29.6 14.0 %collective-permute-start.5 = (f32[128,1024]{1,0:T(8,128)S(1)}, f32[128,1024]{1,0:T(8,128)S(1)}, u32[]{:S(2)}, u32[]{:S(2)}) collective-permute-start(f32[128,1024]{1,0:T(8,128)S(1)} %mix_mine.1.left_ref), channel_id=1, source_target_pairs={{0,2},{1,3},{2,0},{3,1},{4,6},{5,7},{6,4},{7,5},{8,10},{9,11},{10,... | collective-permute-start | bytes 1572872 | tf_op jit(solution)/shard_map/ppermute | solution.py:80
  49.8 9.6 %collective-permute-start.14 = (f32[128,512]{1,0:T(8,128)}, f32[128,512]{1,0:T(8,128)}, u32[]{:S(2)}, u32[]{:S(2)}) collective-permute-start(f32[128,512]{1,0:T(8,128)} %get-tuple-element.92), channel_id=1, source_target_pairs={{0,4},{4,0},{8,12},{12,8},{16,20},{20,16},{24,28},{28,24},{1,5},{5... | collective-permute-start | bytes 786440 | tf_op jit(solution)/shard_map/ppermute | solution.py:80
  54.2 18.3 %collective-permute-start.13 = (f32[256,512]{1,0:T(8,128)S(1)}, f32[256,512]{1,0:T(8,128)}, u32[]{:S(2)}, u32[]{:S(2)}) collective-permute-start(f32[256,512]{1,0:T(8,128)S(1)} %get-tuple-element.84.refs_3_), channel_id=1, source_target_pairs={{0,8},{4,12},{8,0},{12,4},{16,24},{20,28},{24,16},{28,20},{1,9},{5... | collective-permute-start | bytes 1572872 | tf_op jit(solution)/shard_map/ppermute | solution.py:80
  54.7 19.4 %collective-permute-start.18 = (f32[256,512]{1,0:T(8,128)}, f32[256,512]{1,0:T(8,128)}, u32[]{:S(2)}, u32[]{:S(2)}) collective-permute-start(f32[256,512]{1,0:T(8,128)} %get-tuple-element.89.up_cot_ref.refs_3_), channel_id=1, source_target_pairs={{0,4},{4,0},{8,12},{12,8},{16,20},{20,16},{24,28},{28,24},{1,5},{5... | collective-permute-start | bytes 1572872 | tf_op jit(solution)/shard_map/ppermute | solution.py:80
  57.9 16.2 %collective-permute-start.12 = (f32[128,1024]{1,0:T(8,128)}, f32[128,1024]{1,0:T(8,128)}, u32[]{:S(2)}, u32[]{:S(2)}) collective-permute-start(f32[128,1024]{1,0:T(8,128)} %feed_mine.1.left_ref), channel_id=1, source_target_pairs={{0,2},{1,3},{2,0},{3,1},{4,6},{5,7},{6,4},{7,5},{8,10},{9,11},{10,... | collective-permute-start | bytes 1572872 | tf_op jit(solution)/shard_map/ppermute | solution.py:80
  65.2 11.3 %collective-permute-start.9 = (f32[128,1024]{1,0:T(8,128)}, f32[128,1024]{1,0:T(8,128)}, u32[]{:S(2)}, u32[]{:S(2)}) collective-permute-start(f32[128,1024]{1,0:T(8,128)} %fusion.29), channel_id=1, source_target_pairs={{0,1},{1,0},{2,3},{3,2},{4,5},{5,4},{6,7},{7,6},{8,9},{9,8},{10,11... | collective-permute-start | bytes 1572872 | tf_op jit(solution)/shard_map/ppermute | solution.py:80
  65.7 65.1 %collective-permute-start.28 = (f32[128,512]{1,0:T(8,128)}, f32[128,512]{1,0:T(8,128)S(1)}, u32[]{:S(2)}, u32[]{:S(2)}) collective-permute-start(f32[128,512]{1,0:T(8,128)} %copy-done.21), channel_id=1, source_target_pairs={{0,1},{1,0},{2,3},{3,2},{4,5},{5,4},{6,7},{7,6},{8,9},{9,8},{10,11... | collective-permute-start | bytes 786440 | tf_op jit(solution)/shard_map/ppermute | solution.py:80
  72.5 13.3 %collective-permute-start.23 = (f32[256,512]{1,0:T(8,128)}, f32[256,512]{1,0:T(8,128)S(1)}, u32[]{:S(2)}, u32[]{:S(2)}) collective-permute-start(f32[256,512]{1,0:T(8,128)} %copy-done.17), channel_id=1, source_target_pairs={{0,8},{4,12},{8,0},{12,4},{16,24},{20,28},{24,16},{28,20},{1,9},{5... | collective-permute-start | bytes 1572872 | tf_op jit(solution)/shard_map/ppermute | solution.py:80
  78.0 20.4 %collective-permute-start.10 = (f32[128,1024]{1,0:T(8,128)S(1)}, f32[128,1024]{1,0:T(8,128)S(1)}, u32[]{:S(2)}, u32[]{:S(2)}) collective-permute-start(f32[128,1024]{1,0:T(8,128)S(1)} %convolution_add_fusion.2.left_ref), channel_id=1, source_target_pairs={{0,2},{1,3},{2,0},{3,1},{4,6},{5,7},{6,4},{7,5},{8,10},{9,11},{10,... | collective-permute-start | bytes 1572872 | tf_op jit(solution)/shard_map/ppermute | solution.py:80
  91.8 14.4 %collective-permute-start.33 = (f32[256,512]{1,0:T(8,128)S(1)}, f32[256,512]{1,0:T(8,128)S(1)}, u32[]{:S(2)}, u32[]{:S(2)}) collective-permute-start(f32[256,512]{1,0:T(8,128)S(1)} %pair_product.18.rest_0_), channel_id=1, source_target_pairs={{0,8},{4,12},{8,0},{12,4},{16,24},{20,28},{24,16},{28,20},{1,9},{5... | collective-permute-start | bytes 1572872 | tf_op jit(solution)/shard_map/ppermute | solution.py:80
  92.4 32.6 %collective-permute-start.36 = (f32[256,512]{1,0:T(8,128)S(1)}, f32[256,512]{1,0:T(8,128)S(1)}, u32[]{:S(2)}, u32[]{:S(2)}) collective-permute-start(f32[256,512]{1,0:T(8,128)S(1)} %pair_product.19.rest_0_), channel_id=1, source_target_pairs={{0,4},{4,0},{8,12},{12,8},{16,20},{20,16},{24,28},{28,24},{1,5},{5... | collective-permute-start | bytes 1572872 | tf_op jit(solution)/shard_map/ppermute | solution.py:80
  92.9 19.8 %collective-permute-start.25 = (f32[128,512]{1,0:T(8,128)S(1)}, f32[128,512]{1,0:T(8,128)S(1)}, u32[]{:S(2)}, u32[]{:S(2)}) collective-permute-start(f32[128,512]{1,0:T(8,128)S(1)} %get-tuple-element.113), channel_id=1, source_target_pairs={{0,4},{4,0},{8,12},{12,8},{16,20},{20,16},{24,28},{28,24},{1,5},{5... | collective-permute-start | bytes 786440 | tf_op jit(solution)/shard_map/ppermute | solution.py:80
  98.4 14.7 %collective-permute-start.24 = (f32[128,1024]{1,0:T(8,128)S(1)}, f32[128,1024]{1,0:T(8,128)S(1)}, u32[]{:S(2)}, u32[]{:S(2)}) collective-permute-start(f32[128,1024]{1,0:T(8,128)S(1)} %add_halves.6.mine_ref), channel_id=1, source_target_pairs={{0,1},{1,0},{2,3},{3,2},{4,5},{5,4},{6,7},{7,6},{8,9},{9,8},{10,11... | collective-permute-start | bytes 1572872 | tf_op jit(solution)/shard_map/ppermute | solution.py:80
  106.2 22.6 %collective-permute-start.35 = (f32[256,768]{1,0:T(8,128)S(1)}, f32[256,768]{1,0:T(8,128)S(1)}, u32[]{:S(2)}, u32[]{:S(2)}) collective-permute-start(f32[256,768]{1,0:T(8,128)S(1)} %get-tuple-element.192.refs_3_), channel_id=1, source_target_pairs={{0,4},{4,0},{8,12},{12,8},{16,20},{20,16},{24,28},{28,24},{1,5},{5... | collective-permute-start | bytes 2359304 | tf_op jit(solution)/shard_map/ppermute | solution.py:80
  122.0 25.2 %collective-permute-start.41 = (f32[128,512]{1,0:T(8,128)S(1)}, f32[128,512]{1,0:T(8,128)S(1)}, u32[]{:S(2)}, u32[]{:S(2)}) collective-permute-start(f32[128,512]{1,0:T(8,128)S(1)} %copy-done.24), channel_id=1, source_target_pairs={{0,1},{1,0},{2,3},{3,2},{4,5},{5,4},{6,7},{7,6},{8,9},{9,8},{10,11... | collective-permute-start | bytes 786440 | tf_op jit(solution)/shard_map/ppermute | solution.py:80
  122.1 28.1 %collective-permute-start.40 = (f32[128,512]{1,0:T(8,128)S(1)}, f32[128,512]{1,0:T(8,128)S(1)}, u32[]{:S(2)}, u32[]{:S(2)}) collective-permute-start(f32[128,512]{1,0:T(8,128)S(1)} %pair_product.20.refs_5_), channel_id=1, source_target_pairs={{0,16},{4,20},{8,24},{12,28},{16,0},{20,4},{24,8},{28,12},{1,17},{... | collective-permute-start | bytes 786440 | tf_op jit(solution)/shard_map/ppermute | solution.py:80
  124.9 18.7 %collective-permute-start.34 = (f32[512,256]{1,0:T(8,128)S(1)}, f32[512,256]{1,0:T(8,128)S(1)}, u32[]{:S(2)}, u32[]{:S(2)}) collective-permute-start(f32[512,256]{1,0:T(8,128)S(1)} %pair_product.21.refs_6_), channel_id=1, source_target_pairs={{0,8},{4,12},{8,0},{12,4},{16,24},{20,28},{24,16},{28,20},{1,9},{5... | collective-permute-start | bytes 1572872 | tf_op jit(solution)/shard_map/ppermute | solution.py:80
  128.9 16.1 %collective-permute-start.31 = (f32[272,384]{1,0:T(8,128)S(1)}, f32[272,384]{1,0:T(8,128)S(1)}, u32[]{:S(2)}, u32[]{:S(2)}) collective-permute-start(f32[272,384]{1,0:T(8,128)S(1)} %few.1.refs_7_.refs_3_), channel_id=1, source_target_pairs={{0,4},{4,0},{8,12},{12,8},{16,20},{20,16},{24,28},{28,24},{1,5},{5... | collective-permute-start | bytes 1253384 | tf_op jit(solution)/shard_map/ppermute | solution.py:80
  130.8 60.2 %collective-permute-start.27 = (f32[128,1024]{1,0:T(8,128)S(1)}, f32[128,1024]{1,0:T(8,128)S(1)}, u32[]{:S(2)}, u32[]{:S(2)}) collective-permute-start(f32[128,1024]{1,0:T(8,128)S(1)} %add.77.left_ref), channel_id=1, source_target_pairs={{0,2},{1,3},{2,0},{3,1},{4,6},{5,7},{6,4},{7,5},{8,10},{9,11},{10,... | collective-permute-start | bytes 1572872 | tf_op jit(solution)/shard_map/ppermute | solution.py:80
  143.7 15.3 %collective-permute-start.39 = (f32[128,512]{1,0:T(8,128)S(1)}, f32[128,512]{1,0:T(8,128)S(1)}, u32[]{:S(2)}, u32[]{:S(2)}) collective-permute-start(f32[128,512]{1,0:T(8,128)S(1)} %pair_product.22.refs_5_), channel_id=1, source_target_pairs={{0,16},{4,20},{8,24},{12,28},{16,0},{20,4},{24,8},{28,12},{1,17},{... | collective-permute-start | bytes 786440 | tf_op jit(solution)/shard_map/ppermute | solution.py:80
  145.0 30.8 %collective-permute-start.38 = (f32[256,768]{1,0:T(8,128)S(1)}, f32[256,768]{1,0:T(8,128)S(1)}, u32[]{:S(2)}, u32[]{:S(2)}) collective-permute-start(f32[256,768]{1,0:T(8,128)S(1)} %pair_product.23.refs_6_), channel_id=1, source_target_pairs={{0,8},{4,12},{8,0},{12,4},{16,24},{20,28},{24,16},{28,20},{1,9},{5... | collective-permute-start | bytes 2359304 | tf_op jit(solution)/shard_map/ppermute | solution.py:80
  147.3 45.3 %collective-permute-start.45 = (f32[512,128]{1,0:T(8,128)S(1)}, f32[512,128]{1,0:T(8,128)S(1)}, u32[]{:S(2)}, u32[]{:S(2)}) collective-permute-start(f32[512,128]{1,0:T(8,128)S(1)} %pair_product.24.refs_5_), channel_id=1, source_target_pairs={{0,16},{4,20},{8,24},{12,28},{16,0},{20,4},{24,8},{28,12},{1,17},{... | collective-permute-start | bytes 786440 | tf_op jit(solution)/shard_map/ppermute | solution.py:80
  150.2 40.3 %collective-permute-start.37 = (f32[272,384]{1,0:T(8,128)S(1)}, f32[272,384]{1,0:T(8,128)S(1)}, u32[]{:S(2)}, u32[]{:S(2)}) collective-permute-start(f32[272,384]{1,0:T(8,128)S(1)} %pair_product.25.refs_5_), channel_id=1, source_target_pairs={{0,8},{4,12},{8,0},{12,4},{16,24},{20,28},{24,16},{28,20},{1,9},{5... | collective-permute-start | bytes 1253384 | tf_op jit(solution)/shard_map/ppermute | solution.py:80
  159.0 32.1 %collective-permute-start.46 = (f32[512,256]{1,0:T(8,128)S(1)}, f32[512,256]{1,0:T(8,128)S(1)}, u32[]{:S(2)}, u32[]{:S(2)}) collective-permute-start(f32[512,256]{1,0:T(8,128)S(1)} %pair_product.26.refs_7_), channel_id=1, source_target_pairs={{0,4},{4,0},{8,12},{12,8},{16,20},{20,16},{24,28},{28,24},{1,5},{5... | collective-permute-start | bytes 1572872 | tf_op jit(solution)/shard_map/ppermute | solution.py:80
  176.1 30.2 %collective-permute-start.44 = (f32[128,768]{1,0:T(8,128)S(1)}, f32[128,768]{1,0:T(8,128)S(1)}, u32[]{:S(2)}, u32[]{:S(2)}) collective-permute-start(f32[128,768]{1,0:T(8,128)S(1)} %pair_product.29.refs_6_), channel_id=1, source_target_pairs={{0,16},{4,20},{8,24},{12,28},{16,0},{20,4},{24,8},{28,12},{1,17},{... | collective-permute-start | bytes 1179656 | tf_op jit(solution)/shard_map/ppermute | solution.py:80
  190.9 20.1 %collective-permute-start.43 = (f32[144,384]{1,0:T(8,128)S(1)}, f32[144,384]{1,0:T(8,128)S(1)}, u32[]{:S(2)}, u32[]{:S(2)}) collective-permute-start(f32[144,384]{1,0:T(8,128)S(1)} %pair_product.30.rest_0_), channel_id=1, source_target_pairs={{0,16},{4,20},{8,24},{12,28},{16,0},{20,4},{24,8},{28,12},{1,17},{... | collective-permute-start | bytes 663560 | tf_op jit(solution)/shard_map/ppermute | solution.py:80
  191.0 31.2 %collective-permute-start.42 = (f32[128,1024]{1,0:T(8,128)S(1)}, f32[128,1024]{1,0:T(8,128)}, u32[]{:S(2)}, u32[]{:S(2)}) collective-permute-start(f32[128,1024]{1,0:T(8,128)S(1)} %add_halves.7.mine_ref.refs_6_), channel_id=1, source_target_pairs={{0,1},{1,0},{2,3},{3,2},{4,5},{5,4},{6,7},{7,6},{8,9},{9,8},{10,11... | collective-permute-start | bytes 1572872 | tf_op jit(solution)/shard_map/ppermute | solution.py:80
  194.2 21.0 %collective-permute-start.50 = (f32[512,128]{1,0:T(8,128)S(1)}, f32[512,128]{1,0:T(8,128)S(1)}, u32[]{:S(2)}, u32[]{:S(2)}) collective-permute-start(f32[512,128]{1,0:T(8,128)S(1)} %pair_product.31.refs_7_), channel_id=1, source_target_pairs={{0,16},{4,20},{8,24},{12,28},{16,0},{20,4},{24,8},{28,12},{1,17},{... | collective-permute-start | bytes 786440 | tf_op jit(solution)/shard_map/ppermute | solution.py:80
  (105 other events, 370.8 us)
where the time goes:
time: 226 us; the launch traced here: 225 us
  waiting for transfers between devices  99.1 us (44%)
  Pallas kernels  45.6 us (20%)
  starting transfers between devices  44.5 us (20%)
  local copies, waits for them, and re-layouts  17.3 us (8%)
  matrix products  8.88 us (4%)
  other arithmetic  7.27 us (3%)
    ppermute x51, waiting for transfers between devices, swap(): return lax.ppermute(values, axis, pairs)  99.1 us
    ppermute x51, starting transfers between devices, swap(): return lax.ppermute(values, axis, pairs)  44.5 us
    pallas_call x38, Pallas kernels, call(): pl.pallas_call(kernel, grid=(1,), in_specs=[place(value) for value in val...  40.2 us
    unnamed x176, local copies, waits for them, and re-layouts  12.7 us
    dot_general x9, matrix products, dot(): lax.dot_general(left, right, ((dims[:1], dims[1:]), ((), ())), precision=...  6.01 us
    pallas_call x5, Pallas kernels, arrange(): pl.pallas_call(functools.partial(arrange_kernel, order, pair, width), in_...  5.36 us
  transfers between devices with their start and end apart: 51, of which 24 were waited for; matrix products, arithmetic and copies ran while one was open for 8% of the time, Pallas kernels for 17%

commit v1 on v0

--- a/solution.py
+++ b/solution.py
@@ -13,7 +13,7 @@
 HEAD_PAD = 128
 STATE_ROWS = 18
 STATE_PAD = 24
-SMALL_ROWS = 16
+SMALL_ROWS = 48
 COST = 3 * 10**9
 
 epsilon = 1e-05
@@ -732,34 +732,28 @@
 
 
 def few_kernel(
-    core_ref, me_ref, near_ref, far_own_ref, far_ref, bc_ref, kv_ref, q_ref, dt_ref, gain_two_ref,
-    taps_ref, gain_ref, heads_ref, *rest
+    core_ref, me_ref, near_ref, far_own_ref, far_ref, bc_ref, kv_ref, gain_two_ref, taps_ref,
+    gain_ref, heads_ref, *rest
 ):
     few_ref = rest[-1]
     tokens = bc_ref.shape[0]
     blocks = shared_blocks(bc_ref, kv_ref)
-    few_ref[:tokens, :128] = q_ref[...]
-    few_ref[:tokens, 128:256] = (
-        pick(me_ref[0], blocks) + near_ref[:tokens, :] + far_ref[:tokens, :]
-    )
-    few_ref[:tokens, 256:] = dt_ref[...]
+    few_ref[:tokens, :] = pick(me_ref[0], blocks) + near_ref[:tokens, :] + far_ref[:tokens, :]
     state = far_own_ref[tokens:, :] + far_ref[tokens:, :]
     used = STATE_ROWS
     few_ref[tokens:, :] = jnp.zeros((few_ref.shape[0] - tokens, few_ref.shape[1]), f32)
     values = (state[:used], gain_two_ref[...], taps_ref[...], gain_ref[...], heads_ref[...])
     for at, (value, row, start) in enumerate(chunks(values)):
-        place = tokens + at // 3
-        cols = slice(at % 3 * 128, at % 3 * 128 + 128)
-        few_ref[place : place + 1, cols] = value[row : row + 1, start : start + 128]
+        place = tokens + at
+        few_ref[place : place + 1, :] = value[row : row + 1, start : start + 128]
 
 
 def unpack_kernel(core_ref, few_ref, own_ref, *refs):
     rows_out = own_ref.shape[0]
-    own_ref[...] = few_ref[:rows_out, 128:256]
+    own_ref[...] = few_ref[:rows_out, :]
     for at, (ref, row, start) in enumerate(chunks(refs)):
-        place = rows_out + at // 3
-        cols = slice(at % 3 * 128, at % 3 * 128 + 128)
-        ref[row : row + 1, start : start + 128] = few_ref[place : place + 1, cols]
+        place = rows_out + at
+        ref[row : row + 1, start : start + 128] = few_ref[place : place + 1, :]
 
 
 def assemble_kernel(core_ref, me_ref, own_ref, near_ref, far_ref, far_near_ref, bc_ref, *kv_refs):
@@ -1002,7 +996,7 @@
         (me_arg, normed_grad, hidden, taps_bc_grad, bc_cot, kv_cot),
         (mix_pair[1],),
     )
-    zx_own = jnp.concatenate([z_cot, x_cot], axis=1)
+    zx_own = jnp.concatenate([z_cot, x_cot, q_cot, dt_cot], axis=1)
     zx_got = swap(zx_own, "dp", 1)
     zx_stages = halving(normed_pair, (zx_own, zx_got), True)
     near = swap(near, "tensor", 1)
@@ -1017,11 +1011,11 @@
     (few,) = call_dense(
         few_kernel,
         "few",
-        [((tokens + SMALL_ROWS, 384), f32)],
+        [((tokens + SMALL_ROWS, 128), f32)],
         core_arg,
         (
-            me_arg, near, far_own, far, bc_cot, kv_cot, q_cot, dt_cot, norm_two_grad, taps_x_grad,
-            gain_grad, heads_grad,
+            me_arg, near, far_own, far, bc_cot, kv_cot, norm_two_grad, taps_x_grad, gain_grad,
+            heads_grad,
         ),
     )
     few_got = swap(few, "dp", 1)
@@ -1051,20 +1045,20 @@
     last = advance("mix", last, far_own)
     last = advance("gate", last, zx_got)
     last = advance("zx", last)
-    last = advance("mix", last, few)
-    last = advance("few", last)
-    last = advance("down", last)
-    last = advance("up", last)
-    last = advance("gate", last)
-    last = advance("zx", last)
-    last = advance("few", last)
+    last = advance("few", last, few)
     normed_mine, normed_other = tensor_halves(normed_mine, (last,))
     last = normed_mine
     last = advance("down", last)
     last = advance("mix", last)
-    last = advance("zx", last)
+    last = advance("up", last)
+    last = advance("gate", last)
     last = advance("few", last)
     last = advance("down", last)
+    last = advance("zx", last)
+    last = advance("mix", last)
+    last = advance("few", last)
+    last = advance("down", last)
+    last = advance("zx", last)
     (input_grad,) = call_dense(
         input_grad_kernel,
         "input_grad",
@@ -1087,11 +1081,12 @@
     down_shard, mixed_shard = totals["down"], totals["mix"]
     out_shard, o_shard = mixed_shard[:inner_cols], mixed_shard[inner_cols:]
     gu_shard = jnp.stack([totals["gate"], totals["up"]], axis=1)
-    zx_shard = totals["zx"].reshape(-1, 2, inner_cols)
+    zx_total = totals["zx"]
+    zx_shard = zx_total[:, : 2 * inner_cols].reshape(-1, 2, inner_cols)
     few_shard = totals["few"]
     shard_rows = model // lax.axis_size("dp")
-    q_shard = few_shard[:shard_rows, :query_cols]
-    dt_shard = few_shard[:shard_rows, 256 : 256 + head_count]
+    q_shard = zx_total[:, 2 * inner_cols : 2 * inner_cols + query_cols]
+    dt_shard = zx_total[:, 2 * inner_cols + query_cols :][:, :head_count]
     own, norm_one_grad, state_grad, norm_two_grad, inner_grad, gain_grad, heads_grad = call_dense(
         unpack_kernel,
         "unpack",

time: 226 us -> 221 us (0.978)
  waiting for transfers between devices: 99.1 us -> 96.2 us
  other arithmetic: 7.27 us -> 4.76 us
    ppermute x51, waiting for transfers between devices: 99.1 us -> 96.2 us  [swap(): return lax.ppermute(values, axis, pairs)]
    unnamed x176 -> x193, local copies, waits for them, and re-layouts: 12.7 us -> 12 us
  transfers between devices with their start and end apart: 51 -> 51, of which waited for: 24 -> 21; matrix products, arithmetic and copies ran while one was open for 8% -> 7% of each run, Pallas kernels for 17% -> 18%
where the time goes in v1:
time: 221 us; the launch traced here: 220 us
  waiting for transfers between devices  96.2 us (44%)
  starting transfers between devices  45.5 us (21%)
  Pallas kernels  45.2 us (20%)
  local copies, waits for them, and re-layouts  16 us (7%)
  matrix products  10.7 us (5%)
  other arithmetic  4.76 us (2%)
    ppermute x51, waiting for transfers between devices, swap(): return lax.ppermute(values, axis, pairs)  96.2 us
    ppermute x51, starting transfers between devices, swap(): return lax.ppermute(values, axis, pairs)  45.5 us
    pallas_call x38, Pallas kernels, call(): pl.pallas_call(kernel, grid=(1,), in_specs=[place(value) for value in val...  39.9 us
    unnamed x193, local copies, waits for them, and re-layouts  12 us
    dot_general x9, matrix products, dot(): lax.dot_general(left, right, ((dims[:1], dims[1:]), ((), ())), precision=...  6.91 us
    pallas_call x5, Pallas kernels, arrange(): pl.pallas_call(functools.partial(arrange_kernel, order, pair, width), in_...  5.35 us
  transfers between devices with their start and end apart: 51, of which 21 were waited for; matrix products, arithmetic and copies ran while one was open for 7% of the time, Pallas kernels for 18%

profile of v1, /device:TPU:0, one launch (start us, length us, event | category | flops | bytes accessed | tf_op | source)
XLA Modules:
  0.0 220.5 jit_solution(8229735744620956083)
XLA Ops:
  7.6 1.9 scan_forward.1
  12.2 2.5 %collective-permute-start.1 = (f32[1,256]{1,0:T(1,128)S(1)}, f32[1,256]{1,0:T(1,128)}, u32[]{:S(2)}, u32[]{:S(2)}) collective-permute-start(f32[1,256]{1,0:T(1,128)S(1)} %get-tuple-element.79.sq_a), channel_id=1, source_target_pairs={{0,2},{1,3},{2,0},{3,1},{4,6},{5,7},{6,4},{7,5},{8,10},{9,11},{10,... | collective-permute-start | bytes 3080 | tf_op jit(solution)/shard_map/ppermute | solution.py:80
  16.3 1.7 collective-permute-start.3
  26.4 1.8 collective-permute-start.7
  28.6 1.8 collective-permute-start.5
  33.7 5.6 %collective-permute-done.6.rest_0_.refs_1_ = f32[128,512]{1,0:T(8,128)S(1)} collective-permute-done((f32[128,512]{1,0:T(8,128)S(1)}, f32[128,512]{1,0:T(8,128)S(1)}, u32[]{:S(2)}, u32[]{:S(2)}) %collective-permute-start.6) | collective-permute-done | bytes 262176 | tf_op jit(solution)/shard_map/ppermute | solution.py:80
  40.7 2.0 collective-permute-done.5.right_ref
  42.9 1.9 collective-permute-done.8.got_ref
  44.8 1.9 feed.1
  46.8 1.8 collective-permute-start.13
  54.3 2.7 %feed_mine.1.left_ref = f32[128,1024]{1,0:T(8,128)} custom-call(s32[1]{0:T(128)} %bitcast.core_ref, f32[256,512]{1,0:T(8,128)S(1)} %get-tuple-element.88.gate_cot_ref.refs_3_, f32[256,512]{1,0:T(8,128)} %get-tuple-element.89.up_cot_ref.refs_3_, bf16[2,1024,512]{2,1,0:T(8,128)(2,1)S(1)} %bitcast.66, f32[128,1024]{1,0:T(8,128)S(1)} %collective-permute-done.11.got_ref), custom_call_target="tpu_custom_call" | custom-call | flops 3000000000 | bytes 1000000 | tf_op jit(solution)/shard_map/feed_mine/pallas_call | solution.py:64
  57.0 1.7 collective-permute-start.12
  60.2 6.6 %collective-permute-done.16.rest_3_.refs_1_ = f32[128,512]{1,0:T(8,128)} collective-permute-done((f32[128,512]{1,0:T(8,128)}, f32[128,512]{1,0:T(8,128)}, u32[]{:S(2)}, u32[]{:S(2)}) %collective-permute-start.16) | collective-permute-done | bytes 262176 | tf_op jit(solution)/shard_map/ppermute | solution.py:80
  66.8 2.3 %fusion.29 = f32[128,1024]{1,0:T(8,128)} fusion(bf16[512,1024]{1,0:T(8,128)(2,1)} %param.39, bf16[256,512]{1,0:T(8,128)(2,1)S(1)} %convert_element_type.33, s32[]{:T(128)S(6)} %select_n.66), kind=kOutput, calls=%fused_computation.42 | convolution fusion | flops 134217728 | bytes 1703940 | tf_op jit(solution)/shard_map/dot_general | solution.py:28
  70.4 1.8 collective-permute-start.23
  77.8 1.8 pair_product.18.rest_0_
  82.7 2.2 %collective-permute-done.23.refs_4_ = f32[256,512]{1,0:T(8,128)S(1)} collective-permute-done((f32[256,512]{1,0:T(8,128)}, f32[256,512]{1,0:T(8,128)S(1)}, u32[]{:S(2)}, u32[]{:S(2)}) %collective-permute-start.23) | collective-permute-done | bytes 524320 | tf_op jit(solution)/shard_map/ppermute | solution.py:80
  93.0 3.9 %scan_backward.1 = (f32[256,384]{1,0:T(8,128)S(1)}, f32[256,384]{1,0:T(8,128)S(1)}, f32[256,256]{1,0:T(8,128)S(1)}, f32[256,128]{1,0:T(8,128)S(1)}, f32[5,384]{1...) custom-call(f32[2,256,384]{2,1,0:T(8,128)S(1)} %copy-done.48, ...), custom_call_target="tpu_custom_call" | custom-call | flops 3000000000 | bytes 1000000 | tf_op jit(solution)/shard_map/scan_backward/pallas_call | solution.py:64
  100.4 3.6 %collective-permute-done.35.refs_5_ = f32[256,512]{1,0:T(8,128)S(1)} collective-permute-done((f32[256,512]{1,0:T(8,128)S(1)}, f32[256,512]{1,0:T(8,128)S(1)}, u32[]{:S(2)}, u32[]{:S(2)}) %collective-permute-start.35) | collective-permute-done | bytes 524320 | tf_op jit(solution)/shard_map/ppermute | solution.py:80
  107.1 4.2 %collective-permute-done.25.rest_0_.refs_1_ = f32[128,512]{1,0:T(8,128)S(1)} collective-permute-done((f32[128,512]{1,0:T(8,128)S(1)}, f32[128,512]{1,0:T(8,128)S(1)}, u32[]{:S(2)}, u32[]{:S(2)}) %collective-permute-start.25) | collective-permute-done | bytes 262176 | tf_op jit(solution)/shard_map/ppermute | solution.py:80
  117.0 4.3 %collective-permute-done.30.far_ref = f32[280,128]{1,0:T(8,128)S(1)} collective-permute-done((f32[280,128]{1,0:T(8,128)S(1)}, f32[280,128]{1,0:T(8,128)S(1)}, u32[]{:S(2)}, u32[]{:S(2)}) %collective-permute-start.30) | collective-permute-done | bytes 143392 | tf_op jit(solution)/shard_map/ppermute | solution.py:80
  121.4 2.6 %collective-permute-start.39 = (f32[128,512]{1,0:T(8,128)S(1)}, f32[128,512]{1,0:T(8,128)S(1)}, u32[]{:S(2)}, u32[]{:S(2)}) collective-permute-start(f32[128,512]{1,0:T(8,128)S(1)} %pair_product.20.refs_5_), channel_id=1, source_target_pairs={{0,16},{4,20},{8,24},{12,28},{16,0},{20,4},{24,8},{28,12},{1,17},{... | collective-permute-start | bytes 786440 | tf_op jit(solution)/shard_map/ppermute | solution.py:80
  124.7 8.8 %collective-permute-done.32.refs_7_.refs_4_ = f32[256,1024]{1,0:T(8,128)S(1)} collective-permute-done((f32[256,1024]{1,0:T(8,128)S(1)}, f32[256,1024]{1,0:T(8,128)S(1)}, u32[]{:S(2)}, u32[]{:S(2)}) %collective-permute-start.32) | collective-permute-done | bytes 1048608 | tf_op jit(solution)/shard_map/ppermute | solution.py:80
  137.4 1.8 collective-permute-done.31.refs_4_
  139.2 2.6 %collective-permute-start.38 = (f32[128,512]{1,0:T(8,128)S(1)}, f32[128,512]{1,0:T(8,128)S(1)}, u32[]{:S(2)}, u32[]{:S(2)}) collective-permute-start(f32[128,512]{1,0:T(8,128)S(1)} %pair_product.22.refs_5_), channel_id=1, source_target_pairs={{0,16},{4,20},{8,24},{12,28},{16,0},{20,4},{24,8},{28,12},{1,17},{... | collective-permute-start | bytes 786440 | tf_op jit(solution)/shard_map/ppermute | solution.py:80
  142.1 7.6 %collective-permute-done.27.right_ref = f32[128,1024]{1,0:T(8,128)S(1)} collective-permute-done((f32[128,1024]{1,0:T(8,128)S(1)}, f32[128,1024]{1,0:T(8,128)S(1)}, u32[]{:S(2)}, u32[]{:S(2)}) %collective-permute-start.27) | collective-permute-done | bytes 524320 | tf_op jit(solution)/shard_map/ppermute | solution.py:80
  154.0 2.6 %collective-permute-start.43 = (f32[512,128]{1,0:T(8,128)S(1)}, f32[512,128]{1,0:T(8,128)S(1)}, u32[]{:S(2)}, u32[]{:S(2)}) collective-permute-start(f32[512,128]{1,0:T(8,128)S(1)} %pair_product.26.refs_7_), channel_id=1, source_target_pairs={{0,16},{4,20},{8,24},{12,28},{16,0},{20,4},{24,8},{28,12},{1,17},{... | collective-permute-start | bytes 786440 | tf_op jit(solution)/shard_map/ppermute | solution.py:80
  162.2 10.1 %collective-permute-done.45.refs_5_ = f32[512,256]{1,0:T(8,128)S(1)} collective-permute-done((f32[512,256]{1,0:T(8,128)S(1)}, f32[512,256]{1,0:T(8,128)S(1)}, u32[]{:S(2)}, u32[]{:S(2)}) %collective-permute-start.45) | collective-permute-done | bytes 524320 | tf_op jit(solution)/shard_map/ppermute | solution.py:80
  175.4 13.1 %collective-permute-done.44.refs_5_ = f32[256,1024]{1,0:T(8,128)S(1)} collective-permute-done((f32[256,1024]{1,0:T(8,128)S(1)}, f32[256,1024]{1,0:T(8,128)S(1)}, u32[]{:S(2)}, u32[]{:S(2)}) %collective-permute-start.44) | collective-permute-done | bytes 1048608 | tf_op jit(solution)/shard_map/ppermute | solution.py:80
  193.4 13.9 %collective-permute-done.47.refs_6_ = f32[512,128]{1,0:T(8,128)S(1)} collective-permute-done((f32[512,128]{1,0:T(8,128)S(1)}, f32[512,128]{1,0:T(8,128)S(1)}, u32[]{:S(2)}, u32[]{:S(2)}) %collective-permute-start.47) | collective-permute-done | bytes 262176 | tf_op jit(solution)/shard_map/ppermute | solution.py:80
  207.3 2.1 pair_product.34.refs_7_
  213.4 4.3 %collective-permute-done.46.refs_6_ = f32[128,1024]{1,0:T(8,128)S(1)} collective-permute-done((f32[128,1024]{1,0:T(8,128)}, f32[128,1024]{1,0:T(8,128)S(1)}, u32[]{:S(2)}, u32[]{:S(2)}) %collective-permute-start.46) | collective-permute-done | bytes 524320 | tf_op jit(solution)/shard_map/ppermute | solution.py:80
  (352 shorter events, 90.5 us)
Async XLA Ops:
  11.7 12.3 %collective-permute-start = (f32[1,256]{1,0:T(1,128)S(1)}, f32[1,256]{1,0:T(1,128)}, u32[]{:S(2)}, u32[]{:S(2)}) collective-permute-start(f32[1,256]{1,0:T(1,128)S(1)} %get-tuple-element.79.sq_a), channel_id=1, source_target_pairs={{0,1},{1,0},{2,3},{3,2},{4,5},{5,4},{6,7},{7,6},{8,9},{9,8},{10,11... | collective-permute-start | bytes 3080 | tf_op jit(solution)/shard_map/ppermute | solution.py:80
  12.2 11.8 %collective-permute-start.1 = (f32[1,256]{1,0:T(1,128)S(1)}, f32[1,256]{1,0:T(1,128)}, u32[]{:S(2)}, u32[]{:S(2)}) collective-permute-start(f32[1,256]{1,0:T(1,128)S(1)} %get-tuple-element.79.sq_a), channel_id=1, source_target_pairs={{0,2},{1,3},{2,0},{3,1},{4,6},{5,7},{6,4},{7,5},{8,10},{9,11},{10,... | collective-permute-start | bytes 3080 | tf_op jit(solution)/shard_map/ppermute | solution.py:80
  26.4 14.3 %collective-permute-start.7 = (f32[256,512]{1,0:T(8,128)S(1)}, f32[256,512]{1,0:T(8,128)S(1)}, u32[]{:S(2)}, u32[]{:S(2)}) collective-permute-start(f32[256,512]{1,0:T(8,128)S(1)} %get-tuple-element.81.mixed_ref.refs_3_), channel_id=1, source_target_pairs={{0,4},{4,0},{8,12},{12,8},{16,20},{20,16},{24,28},{28,24},{1,5},{5... | collective-permute-start | bytes 1572872 | tf_op jit(solution)/shard_map/ppermute | solution.py:80
  28.6 14.1 %collective-permute-start.5 = (f32[128,1024]{1,0:T(8,128)S(1)}, f32[128,1024]{1,0:T(8,128)S(1)}, u32[]{:S(2)}, u32[]{:S(2)}) collective-permute-start(f32[128,1024]{1,0:T(8,128)S(1)} %mix_mine.1.left_ref), channel_id=1, source_target_pairs={{0,2},{1,3},{2,0},{3,1},{4,6},{5,7},{6,4},{7,5},{8,10},{9,11},{10,... | collective-permute-start | bytes 1572872 | tf_op jit(solution)/shard_map/ppermute | solution.py:80
  46.8 23.6 %collective-permute-start.13 = (f32[256,512]{1,0:T(8,128)S(1)}, f32[256,512]{1,0:T(8,128)}, u32[]{:S(2)}, u32[]{:S(2)}) collective-permute-start(f32[256,512]{1,0:T(8,128)S(1)} %get-tuple-element.84.refs_3_), channel_id=1, source_target_pairs={{0,8},{4,12},{8,0},{12,4},{16,24},{20,28},{24,16},{28,20},{1,9},{5... | collective-permute-start | bytes 1572872 | tf_op jit(solution)/shard_map/ppermute | solution.py:80
  53.6 13.2 %collective-permute-start.16 = (f32[128,512]{1,0:T(8,128)}, f32[128,512]{1,0:T(8,128)}, u32[]{:S(2)}, u32[]{:S(2)}) collective-permute-start(f32[128,512]{1,0:T(8,128)} %get-tuple-element.93), channel_id=1, source_target_pairs={{0,8},{4,12},{8,0},{12,4},{16,24},{20,28},{24,16},{28,20},{1,9},{5... | collective-permute-start | bytes 786440 | tf_op jit(solution)/shard_map/ppermute | solution.py:80
  54.0 18.2 %collective-permute-start.18 = (f32[256,512]{1,0:T(8,128)}, f32[256,512]{1,0:T(8,128)}, u32[]{:S(2)}, u32[]{:S(2)}) collective-permute-start(f32[256,512]{1,0:T(8,128)} %get-tuple-element.89.up_cot_ref.refs_3_), channel_id=1, source_target_pairs={{0,4},{4,0},{8,12},{12,8},{16,20},{20,16},{24,28},{28,24},{1,5},{5... | collective-permute-start | bytes 1572872 | tf_op jit(solution)/shard_map/ppermute | solution.py:80
  57.0 15.2 %collective-permute-start.12 = (f32[128,1024]{1,0:T(8,128)}, f32[128,1024]{1,0:T(8,128)}, u32[]{:S(2)}, u32[]{:S(2)}) collective-permute-start(f32[128,1024]{1,0:T(8,128)} %feed_mine.1.left_ref), channel_id=1, source_target_pairs={{0,2},{1,3},{2,0},{3,1},{4,6},{5,7},{6,4},{7,5},{8,10},{9,11},{10,... | collective-permute-start | bytes 1572872 | tf_op jit(solution)/shard_map/ppermute | solution.py:80
  70.4 65.9 %collective-permute-start.28 = (f32[128,512]{1,0:T(8,128)}, f32[128,512]{1,0:T(8,128)S(1)}, u32[]{:S(2)}, u32[]{:S(2)}) collective-permute-start(f32[128,512]{1,0:T(8,128)} %copy-done.27), channel_id=1, source_target_pairs={{0,1},{1,0},{2,3},{3,2},{4,5},{5,4},{6,7},{7,6},{8,9},{9,8},{10,11... | collective-permute-start | bytes 786440 | tf_op jit(solution)/shard_map/ppermute | solution.py:80
  70.4 14.5 %collective-permute-start.23 = (f32[256,512]{1,0:T(8,128)}, f32[256,512]{1,0:T(8,128)S(1)}, u32[]{:S(2)}, u32[]{:S(2)}) collective-permute-start(f32[256,512]{1,0:T(8,128)} %copy-done.23), channel_id=1, source_target_pairs={{0,8},{4,12},{8,0},{12,4},{16,24},{20,28},{24,16},{28,20},{1,9},{5... | collective-permute-start | bytes 1572872 | tf_op jit(solution)/shard_map/ppermute | solution.py:80
  76.1 20.8 %collective-permute-start.10 = (f32[128,1024]{1,0:T(8,128)S(1)}, f32[128,1024]{1,0:T(8,128)S(1)}, u32[]{:S(2)}, u32[]{:S(2)}) collective-permute-start(f32[128,1024]{1,0:T(8,128)S(1)} %convolution_add_fusion.2.left_ref), channel_id=1, source_target_pairs={{0,2},{1,3},{2,0},{3,1},{4,6},{5,7},{6,4},{7,5},{8,10},{9,11},{10,... | collective-permute-start | bytes 1572872 | tf_op jit(solution)/shard_map/ppermute | solution.py:80
  89.3 14.8 %collective-permute-start.35 = (f32[256,512]{1,0:T(8,128)S(1)}, f32[256,512]{1,0:T(8,128)S(1)}, u32[]{:S(2)}, u32[]{:S(2)}) collective-permute-start(f32[256,512]{1,0:T(8,128)S(1)} %pair_product.18.rest_0_), channel_id=1, source_target_pairs={{0,8},{4,12},{8,0},{12,4},{16,24},{20,28},{24,16},{28,20},{1,9},{5... | collective-permute-start | bytes 1572872 | tf_op jit(solution)/shard_map/ppermute | solution.py:80
  90.9 33.2 %collective-permute-start.33 = (f32[256,512]{1,0:T(8,128)S(1)}, f32[256,512]{1,0:T(8,128)S(1)}, u32[]{:S(2)}, u32[]{:S(2)}) collective-permute-start(f32[256,512]{1,0:T(8,128)S(1)} %pair_product.19.rest_0_), channel_id=1, source_target_pairs={{0,4},{4,0},{8,12},{12,8},{16,20},{20,16},{24,28},{28,24},{1,5},{5... | collective-permute-start | bytes 1572872 | tf_op jit(solution)/shard_map/ppermute | solution.py:80
  92.4 18.8 %collective-permute-start.25 = (f32[128,512]{1,0:T(8,128)S(1)}, f32[128,512]{1,0:T(8,128)S(1)}, u32[]{:S(2)}, u32[]{:S(2)}) collective-permute-start(f32[128,512]{1,0:T(8,128)S(1)} %get-tuple-element.113), channel_id=1, source_target_pairs={{0,4},{4,0},{8,12},{12,8},{16,20},{20,16},{24,28},{28,24},{1,5},{5... | collective-permute-start | bytes 786440 | tf_op jit(solution)/shard_map/ppermute | solution.py:80
  97.0 14.7 %collective-permute-start.24 = (f32[128,1024]{1,0:T(8,128)S(1)}, f32[128,1024]{1,0:T(8,128)S(1)}, u32[]{:S(2)}, u32[]{:S(2)}) collective-permute-start(f32[128,1024]{1,0:T(8,128)S(1)} %add_halves.6.mine_ref), channel_id=1, source_target_pairs={{0,1},{1,0},{2,3},{3,2},{4,5},{5,4},{6,7},{7,6},{8,9},{9,8},{10,11... | collective-permute-start | bytes 1572872 | tf_op jit(solution)/shard_map/ppermute | solution.py:80
  104.0 29.4 %collective-permute-start.32 = (f32[256,1024]{1,0:T(8,128)S(1)}, f32[256,1024]{1,0:T(8,128)S(1)}, u32[]{:S(2)}, u32[]{:S(2)}) collective-permute-start(f32[256,1024]{1,0:T(8,128)S(1)} %constant_dynamic-update-slice_fusion.refs_3_), channel_id=1, source_target_pairs={{0,4},{4,0},{8,12},{12,8},{16,20},{20,16},{24,28},{28,24},{1,5},{5... | collective-permute-start | bytes 3145736 | tf_op jit(solution)/shard_map/ppermute | solution.py:80
  121.3 28.9 %collective-permute-start.41 = (f32[128,512]{1,0:T(8,128)S(1)}, f32[128,512]{1,0:T(8,128)S(1)}, u32[]{:S(2)}, u32[]{:S(2)}) collective-permute-start(f32[128,512]{1,0:T(8,128)S(1)} %copy-done.30), channel_id=1, source_target_pairs={{0,1},{1,0},{2,3},{3,2},{4,5},{5,4},{6,7},{7,6},{8,9},{9,8},{10,11... | collective-permute-start | bytes 786440 | tf_op jit(solution)/shard_map/ppermute | solution.py:80
  121.4 32.6 %collective-permute-start.39 = (f32[128,512]{1,0:T(8,128)S(1)}, f32[128,512]{1,0:T(8,128)S(1)}, u32[]{:S(2)}, u32[]{:S(2)}) collective-permute-start(f32[128,512]{1,0:T(8,128)S(1)} %pair_product.20.refs_5_), channel_id=1, source_target_pairs={{0,16},{4,20},{8,24},{12,28},{16,0},{20,4},{24,8},{28,12},{1,17},{... | collective-permute-start | bytes 786440 | tf_op jit(solution)/shard_map/ppermute | solution.py:80
  124.1 29.1 %collective-permute-start.40 = (f32[512,256]{1,0:T(8,128)S(1)}, f32[512,256]{1,0:T(8,128)S(1)}, u32[]{:S(2)}, u32[]{:S(2)}) collective-permute-start(f32[512,256]{1,0:T(8,128)S(1)} %pair_product.21.refs_6_), channel_id=1, source_target_pairs={{0,8},{4,12},{8,0},{12,4},{16,24},{20,28},{24,16},{28,20},{1,9},{5... | collective-permute-start | bytes 1572872 | tf_op jit(solution)/shard_map/ppermute | solution.py:80
  136.3 13.4 %collective-permute-start.27 = (f32[128,1024]{1,0:T(8,128)S(1)}, f32[128,1024]{1,0:T(8,128)S(1)}, u32[]{:S(2)}, u32[]{:S(2)}) collective-permute-start(f32[128,1024]{1,0:T(8,128)S(1)} %add.77.left_ref), channel_id=1, source_target_pairs={{0,2},{1,3},{2,0},{3,1},{4,6},{5,7},{6,4},{7,5},{8,10},{9,11},{10,... | collective-permute-start | bytes 1572872 | tf_op jit(solution)/shard_map/ppermute | solution.py:80
  139.2 19.0 %collective-permute-start.38 = (f32[128,512]{1,0:T(8,128)S(1)}, f32[128,512]{1,0:T(8,128)S(1)}, u32[]{:S(2)}, u32[]{:S(2)}) collective-permute-start(f32[128,512]{1,0:T(8,128)S(1)} %pair_product.22.refs_5_), channel_id=1, source_target_pairs={{0,16},{4,20},{8,24},{12,28},{16,0},{20,4},{24,8},{28,12},{1,17},{... | collective-permute-start | bytes 786440 | tf_op jit(solution)/shard_map/ppermute | solution.py:80
  149.7 10.5 %collective-permute-start.37 = (f32[304,128]{1,0:T(8,128)S(1)}, f32[304,128]{1,0:T(8,128)S(1)}, u32[]{:S(2)}, u32[]{:S(2)}) collective-permute-start(f32[304,128]{1,0:T(8,128)S(1)} %pair_product.24.rest_0_), channel_id=1, source_target_pairs={{0,8},{4,12},{8,0},{12,4},{16,24},{20,28},{24,16},{28,20},{1,9},{5... | collective-permute-start | bytes 466952 | tf_op jit(solution)/shard_map/ppermute | solution.py:80
  150.2 38.3 %collective-permute-start.44 = (f32[256,1024]{1,0:T(8,128)S(1)}, f32[256,1024]{1,0:T(8,128)S(1)}, u32[]{:S(2)}, u32[]{:S(2)}) collective-permute-start(f32[256,1024]{1,0:T(8,128)S(1)} %pair_product.23.refs_5_), channel_id=1, source_target_pairs={{0,8},{4,12},{8,0},{12,4},{16,24},{20,28},{24,16},{28,20},{1,9},{5... | collective-permute-start | bytes 3145736 | tf_op jit(solution)/shard_map/ppermute | solution.py:80
  153.3 20.8 %collective-permute-start.36 = (f32[128,1024]{1,0:T(8,128)S(1)}, f32[128,1024]{1,0:T(8,128)S(1)}, u32[]{:S(2)}, u32[]{:S(2)}) collective-permute-start(f32[128,1024]{1,0:T(8,128)S(1)} %add_halves.7.mine_ref.refs_5_), channel_id=1, source_target_pairs={{0,1},{1,0},{2,3},{3,2},{4,5},{5,4},{6,7},{7,6},{8,9},{9,8},{10,11... | collective-permute-start | bytes 1572872 | tf_op jit(solution)/shard_map/ppermute | solution.py:80
  154.0 36.3 %collective-permute-start.43 = (f32[512,128]{1,0:T(8,128)S(1)}, f32[512,128]{1,0:T(8,128)S(1)}, u32[]{:S(2)}, u32[]{:S(2)}) collective-permute-start(f32[512,128]{1,0:T(8,128)S(1)} %pair_product.26.refs_7_), channel_id=1, source_target_pairs={{0,16},{4,20},{8,24},{12,28},{16,0},{20,4},{24,8},{28,12},{1,17},{... | collective-permute-start | bytes 786440 | tf_op jit(solution)/shard_map/ppermute | solution.py:80
  158.2 14.1 %collective-permute-start.45 = (f32[512,256]{1,0:T(8,128)S(1)}, f32[512,256]{1,0:T(8,128)S(1)}, u32[]{:S(2)}, u32[]{:S(2)}) collective-permute-start(f32[512,256]{1,0:T(8,128)S(1)} %pair_product.25.refs_6_), channel_id=1, source_target_pairs={{0,4},{4,0},{8,12},{12,8},{16,20},{20,16},{24,28},{28,24},{1,5},{5... | collective-permute-start | bytes 1572872 | tf_op jit(solution)/shard_map/ppermute | solution.py:80
  160.5 30.2 %collective-permute-start.42 = (f32[176,128]{1,0:T(8,128)S(1)}, f32[176,128]{1,0:T(8,128)S(1)}, u32[]{:S(2)}, u32[]{:S(2)}) collective-permute-start(f32[176,128]{1,0:T(8,128)S(1)} %pair_product.29.refs_6_), channel_id=1, source_target_pairs={{0,16},{4,20},{8,24},{12,28},{16,0},{20,4},{24,8},{28,12},{1,17},{... | collective-permute-start | bytes 270344 | tf_op jit(solution)/shard_map/ppermute | solution.py:80
  173.7 33.6 %collective-permute-start.47 = (f32[512,128]{1,0:T(8,128)S(1)}, f32[512,128]{1,0:T(8,128)S(1)}, u32[]{:S(2)}, u32[]{:S(2)}) collective-permute-start(f32[512,128]{1,0:T(8,128)S(1)} %pair_product.30.refs_6_), channel_id=1, source_target_pairs={{0,16},{4,20},{8,24},{12,28},{16,0},{20,4},{24,8},{28,12},{1,17},{... | collective-permute-start | bytes 786440 | tf_op jit(solution)/shard_map/ppermute | solution.py:80
  189.7 28.0 %collective-permute-start.46 = (f32[128,1024]{1,0:T(8,128)}, f32[128,1024]{1,0:T(8,128)S(1)}, u32[]{:S(2)}, u32[]{:S(2)}) collective-permute-start(f32[128,1024]{1,0:T(8,128)} %pair_product.31.refs_7_), channel_id=1, source_target_pairs={{0,16},{4,20},{8,24},{12,28},{16,0},{20,4},{24,8},{28,12},{1,17},{... | collective-permute-start | bytes 1572872 | tf_op jit(solution)/shard_map/ppermute | solution.py:80
  191.6 20.4 %collective-permute-start.48 = (f32[128,128]{1,0:T(8,128)S(1)}, f32[128,128]{1,0:T(8,128)S(1)}, u32[]{:S(2)}, u32[]{:S(2)}) collective-permute-start(f32[128,128]{1,0:T(8,128)S(1)} %get-tuple-element.126.own_ref), channel_id=1, source_target_pairs={{0,1},{1,0},{2,3},{3,2},{4,5},{5,4},{6,7},{7,6},{8,9},{9,8},{10,11... | collective-permute-start | bytes 196616 | tf_op jit(solution)/shard_map/ppermute | solution.py:80
  191.6 20.4 %collective-permute-start.49 = (f32[128,128]{1,0:T(8,128)S(1)}, f32[128,128]{1,0:T(8,128)S(1)}, u32[]{:S(2)}, u32[]{:S(2)}) collective-permute-start(f32[128,128]{1,0:T(8,128)S(1)} %get-tuple-element.126.own_ref), channel_id=1, source_target_pairs={{0,2},{1,3},{2,0},{3,1},{4,6},{5,7},{6,4},{7,5},{8,10},{9,11},{10,... | collective-permute-start | bytes 196616 | tf_op jit(solution)/shard_map/ppermute | solution.py:80
  191.7 20.2 %collective-permute-start.50 = (f32[128,128]{1,0:T(8,128)S(1)}, f32[128,128]{1,0:T(8,128)S(1)}, u32[]{:S(2)}, u32[]{:S(2)}) collective-permute-start(f32[128,128]{1,0:T(8,128)S(1)} %get-tuple-element.126.own_ref), channel_id=1, source_target_pairs={{0,3},{1,2},{2,1},{3,0},{4,7},{5,6},{6,5},{7,4},{8,11},{9,10},{10,... | collective-permute-start | bytes 196616 | tf_op jit(solution)/shard_map/ppermute | solution.py:80
  (113 other events, 627.3 us)
